TPU v7x, 32 devices: a whole 2x2x4 slice. The times are simulated.
32 devices in a mesh: groups: 2 (over x), rows: 16 (over z, y, core).
Axes of the slice: x: 2, y: 2, z: 4, core: 2. Of those that a mesh axis runs over, the one named last changes fastest.
Arguments:
- rhs: float32 [256, 128, 256], P(('groups', 'rows')), parts along dimension 0, may hold values from -6 to 6
- precision: float32 [256, 256], P(('groups', 'rows')), parts along dimension 0, may hold values from 0.25 to 4
- hessian: float32 [256, 256], P(('groups', 'rows')), parts along dimension 0, may hold values from 0.05 to 2
- diag_blocks: bfloat16 [256, 256, 256], P(('groups', 'rows')), parts along dimension 0, may hold values from -0.125 to 0.125
- cond_blocks: bfloat16 [256, 8, 256, 256], P(('groups', 'rows')), parts along dimension 0, may hold values from -0.125 to 0.125
- cond_ids: int32 [256, 8], P(('groups', 'rows')), parts along dimension 0, may hold values from 0 to 127, as said below
- step_alpha: float32 [2, 128], replicated, may hold values from 0.1 to 0.4
- step_beta: float32 [2, 128], replicated, may hold values from 0.2 to 0.8
Outputs:
- solution: float32 [256, 128, 256], P(('groups', 'rows')), parts along dimension 0
- residual: float32 [256, 128, 256], P(('groups', 'rows')), parts along dimension 0
- direction: float32 [256, 128, 256], P(('groups', 'rows')), parts along dimension 0
There are 2 independent parts, one for each index of `groups`. A program takes and returns all parts, laid end to end along the dimension named above; an argument that names none is the same for every part. Nothing has to cross between parts.
Inputs may be any that keep to these rules, and one draw needn't show every extreme that they name: `cond_ids`: group the blocks into owner sets of 8 consecutive ones (owner set g holds blocks g * 8 onward; there are 128 / 8 owner sets, taken as a cycle). Each row lists 8 distinct blocks, none in its own owner set, all in owner sets at cycle distance 1 to 6 from its own. Over the rows of one owner set, at most 2 distinct blocks are listed from any other owner set, and exactly 2 from some.
All inputs are finite; a program needn't handle non-finite values.
Results may differ from a plain program's by a relative error of at most 0.0047.
Values may be sent and summed in bfloat16 or wider, within the bound.
A program may use at most 128 MiB of HBM per device.

v0:
```python
import jax
import jax.numpy as jnp
from jax import lax
from jax.sharding import PartitionSpec as P

CAP = 2
RADIUS = 6
ITERS = 2


def shifted(value, axis, by):
    length = lax.axis_size(axis)
    return lax.ppermute(value, axis, [(i, (i + by) % length) for i in range(length)])


def plan_slots(needed, slot_total):
    blocks_each = needed.shape[1]
    slot_rank = jnp.cumsum(needed.astype(jnp.int32), axis=1) - 1
    matches = needed[:, None, :] & (
        slot_rank[:, None, :] == jnp.arange(slot_total, dtype=jnp.int32)[None, :, None]
    )
    wanted = jnp.sum(
        jnp.where(matches, jnp.arange(blocks_each, dtype=jnp.int32)[None, None, :], 0), axis=2
    )
    return (slot_rank, wanted)


def on_device(rhs, precision, hessian, diag_blocks, cond_blocks, cond_ids, step_alpha, step_beta):
    dev_count = lax.axis_size("rows")
    my_index = lax.axis_index("rows")
    own_blocks = rhs.shape[0]
    cond_count = cond_ids.shape[1]
    point_count = rhs.shape[2]
    block_total = dev_count * own_blocks
    flat_ids = cond_ids.reshape(-1)
    needed = jnp.any(flat_ids[:, None] == jnp.arange(block_total, dtype=jnp.int32)[None, :], axis=0)
    slot_rank, wanted = plan_slots(needed.reshape(dev_count, own_blocks), CAP)
    owner_dev = flat_ids // own_blocks
    rank_of_entry = jnp.take(slot_rank.reshape(-1), flat_ids)
    offset_list = list(range(1, RADIUS + 1)) + [-step for step in range(1, RADIUS + 1)]
    mine = my_index * own_blocks + jnp.arange(own_blocks, dtype=jnp.int32)
    neighbour_lists = [
        shifted(cond_ids, "rows", -offset_list[slot_index]) for slot_index in range(2 * RADIUS)
    ]
    stacked_lists = jnp.stack(neighbour_lists, axis=0).reshape(
        2 * RADIUS, own_blocks * cond_count, 1
    )
    hits = jnp.any(stacked_lists == mine[None, None, :], axis=1)
    unused_rank, near_asked = plan_slots(hits, CAP)
    neighbour_dev = (my_index + jnp.array(offset_list, dtype=jnp.int32) + dev_count) % dev_count
    asked = jnp.zeros((dev_count, CAP), jnp.int32).at[neighbour_dev].set(near_asked)
    offset_array = jnp.array(offset_list, dtype=jnp.int32)
    relative = (owner_dev - my_index + dev_count) % dev_count
    signed_rel = jnp.where(relative <= dev_count // 2, relative, relative - dev_count)
    offset_slot = jnp.where(signed_rel > 0, signed_rel - 1, RADIUS - signed_rel - 1)
    position = offset_slot * CAP + rank_of_entry
    source_dev = (my_index - offset_array + dev_count) % dev_count
    sources_flat = jnp.take(asked, source_dev, axis=0).reshape(-1)
    slot_groups = 2 * RADIUS

    def fetch_blocks(payload):
        arrived = [
            shifted(payload[slot_index], "rows", -offset_list[slot_index])
            for slot_index in range(slot_groups)
        ]
        return jnp.stack(arrived, axis=0)

    def return_terms(payload):
        back = [
            shifted(payload[slot_index], "rows", offset_list[slot_index])
            for slot_index in range(slot_groups)
        ]
        return jnp.stack(back, axis=0)

    solution = jnp.zeros_like(rhs)
    residual = rhs
    direction = rhs
    for iteration in range(ITERS):
        probe_width = direction.shape[1]
        probe_bf = direction.astype(jnp.bfloat16)
        outgoing = jnp.take(probe_bf, sources_flat, axis=0).reshape(
            slot_groups, CAP, probe_width, point_count
        )
        apply_arrived = fetch_blocks(outgoing)
        remote = jnp.take(
            apply_arrived.reshape(slot_groups * CAP, probe_width, point_count), position, axis=0
        )
        remote = remote.reshape(own_blocks, cond_count, probe_width, point_count)
        forward = jnp.einsum(
            "bij,bpj->bpi", diag_blocks, probe_bf, preferred_element_type=jnp.float32
        )
        forward = forward + jnp.einsum(
            "bkij,bkpj->bpi", cond_blocks, remote, preferred_element_type=jnp.float32
        )
        scaled = (precision[:, None, :] * forward).astype(jnp.bfloat16)
        own_part = jnp.einsum(
            "bij,bpi->bpj", diag_blocks, scaled, preferred_element_type=jnp.float32
        )
        partials = jnp.einsum(
            "bkij,bpi->bkpj", cond_blocks, scaled, preferred_element_type=jnp.float32
        )
        summed = jax.ops.segment_sum(
            partials.reshape(own_blocks * cond_count, probe_width, point_count),
            position,
            num_segments=slot_groups * CAP,
        )
        returned = return_terms(summed.reshape(slot_groups, CAP, probe_width, point_count))
        incoming = jax.ops.segment_sum(
            returned.reshape(slot_groups * CAP, probe_width, point_count),
            sources_flat,
            num_segments=own_blocks,
        )
        operator_image = own_part + incoming + hessian[:, None, :] * direction
        alpha_now = step_alpha[iteration][None, :, None]
        solution = solution + alpha_now * direction
        residual = residual - alpha_now * operator_image
        direction = residual + step_beta[iteration][None, :, None] * direction
    return (solution, residual, direction)


def solution(mesh):
    in_specs = (
        P(("groups", "rows"), None, None),
        P(("groups", "rows"), None),
        P(("groups", "rows"), None),
        P(("groups", "rows"), None, None),
        P(("groups", "rows"), None, None, None),
        P(("groups", "rows"), None),
        P(),
        P(),
    )
    out_specs = (
        P(("groups", "rows"), None, None),
        P(("groups", "rows"), None, None),
        P(("groups", "rows"), None, None),
    )
    return jax.shard_map(
        on_device, mesh=mesh, in_specs=in_specs, out_specs=out_specs, check_vma=False
    )
```

profile of v0, /device:TPU:18, one launch (start us, length us, event | category | flops | bytes accessed | tf_op | source)
XLA Modules:
  0.0 355.9 jit_solution(7033260949657512266)
XLA Ops:
  2.4 3.6 %collective-permute-start.3 = (s32[8,8]{1,0:T(8,128)}, s32[8,8]{1,0:T(8,128)S(1)}, u32[]{:S(2)}, u32[]{:S(2)}) collective-permute-start(s32[8,8]{1,0:T(8,128)} %param.19), channel_id=1, source_target_pairs={{0,12},{1,13},{2,14},{3,15},{4,0},{5,1},{6,2},{7,3},{8,4},{9,5},{1... | collective-permute-start | bytes 776 | tf_op jit(solution)/shard_map/ppermute | solution.py:13
  15.1 2.9 collective-permute-start.8
  18.0 3.4 collective-permute-start.9
  23.1 3.6 collective-permute-done.10
  33.3 2.6 collective-permute-start.13
  36.9 2.6 collective-permute-start.16
  40.2 3.6 collective-permute-start.17
  46.7 4.2 %collective-permute-done.16 = bf16[2,128,256]{2,1,0:T(8,128)(2,1)S(1)} collective-permute-done((bf16[2,128,256]{2,1,0:T(8,128)(2,1)}, bf16[2,128,256]{2,1,0:T(8,128)(2,1)S(1)}, u32[]{:S(2)}, u32[]{:S(2)}) %collective-permute-start.16) | collective-permute-done | bytes 131104 | tf_op jit(solution)/shard_map/ppermute | solution.py:13
  50.9 8.4 %collective-permute-done.17 = bf16[2,128,256]{2,1,0:T(8,128)(2,1)S(1)} collective-permute-done((bf16[2,128,256]{2,1,0:T(8,128)(2,1)}, bf16[2,128,256]{2,1,0:T(8,128)(2,1)S(1)}, u32[]{:S(2)}, u32[]{:S(2)}) %collective-permute-start.17) | collective-permute-done | bytes 131104 | tf_op jit(solution)/shard_map/ppermute | solution.py:13
  59.3 5.6 %collective-permute-start.23 = (bf16[2,128,256]{2,1,0:T(8,128)(2,1)S(1)}, bf16[2,128,256]{2,1,0:T(8,128)(2,1)S(1)}, u32[]{:S(2)}, u32[]{:S(2)}) collective-permute-start(bf16[2,128,256]{2,1,0:T(8,128)(2,1)S(1)} %get-tuple-element.50), channel_id=1, source_target_pairs={{0,6},{1,7},{2,8},{3,9},{4,10},{5,11},{6,12},{7,13},{8,14},{9,15},... | collective-permute-start | bytes 393224 | tf_op jit(solution)/shard_map/ppermute | solution.py:13
  67.2 3.2 collective-permute-done.23
  70.4 2.8 gather_fusion.3
  73.2 2.8 broadcast_select_fusion.1
  76.0 6.3 %convolution_bitcast_fusion.1 = f32[8,128,256]{2,1,0:T(8,128)S(1)} fusion(bf16[8,8,128,256]{3,2,1,0:T(8,128)(2,1)S(1)} %bitcast.164, bf16[8,8,256,256]{3,2,1,0:T(8,128)(2,1)} %param.18), kind=kOutput, calls=%fused_computation.16 | convolution fusion | flops 1073741824 | bytes 13631488 | tf_op jit(solution)/shard_map/bkij,bkpj->bpi/dot_general | solution.py:92
  82.8 4.6 %fusion.6 = f32[8,128,8,256]{3,1,2,0:T(8,128)} fusion(bf16[8,8,256,256]{3,2,1,0:T(8,128)(2,1)S(1)} %bitcast.158, bf16[8,128,256]{2,1,0:T(8,128)(2,1)S(1)} %fusion.2), kind=kOutput, calls=%fused_computation.32 | convolution fusion | flops 1073741824 | bytes 17301504 | tf_op jit(solution)/shard_map/bkij,bpi->bkpj/dot_general | solution.py:99
  89.5 19.8 %scatter_fusion = f32[24,128,256]{2,1,0:T(8,128)} fusion(f32[24,128,256]{2,1,0:T(8,128)} %broadcast.302.clone, s32[64]{0:T(128)S(1)} %copy-done.15, f32[64,128,256]{2,1,0:T(8,128)} %bitcast.162), kind=kCustom, calls=%fused_computation.7 | custom fusion | flops 2097152 | bytes 25166080 | tf_op jit(solution)/shard_map/scatter-add | solution.py:102
  111.6 2.3 collective-permute-start.25
  115.0 3.9 %collective-permute-start.27 = (f32[2,128,256]{2,1,0:T(8,128)S(1)}, f32[2,128,256]{2,1,0:T(8,128)S(1)}, u32[]{:S(2)}, u32[]{:S(2)}) collective-permute-start(f32[2,128,256]{2,1,0:T(8,128)S(1)} %get-tuple-element.33), channel_id=1, source_target_pairs={{0,4},{1,5},{2,6},{3,7},{4,8},{5,9},{6,10},{7,11},{8,12},{9,13},{1... | collective-permute-start | bytes 786440 | tf_op jit(solution)/shard_map/ppermute | solution.py:13
  121.7 3.7 %collective-permute-start.30 = (f32[2,128,256]{2,1,0:T(8,128)S(1)}, f32[2,128,256]{2,1,0:T(8,128)S(1)}, u32[]{:S(2)}, u32[]{:S(2)}) collective-permute-start(f32[2,128,256]{2,1,0:T(8,128)S(1)} %get-tuple-element.30), channel_id=1, source_target_pairs={{0,15},{1,0},{2,1},{3,2},{4,3},{5,4},{6,5},{7,6},{8,7},{9,8},{10,9... | collective-permute-start | bytes 786440 | tf_op jit(solution)/shard_map/ppermute | solution.py:13
  125.4 6.5 %collective-permute-start.31 = (f32[2,128,256]{2,1,0:T(8,128)S(1)}, f32[2,128,256]{2,1,0:T(8,128)S(1)}, u32[]{:S(2)}, u32[]{:S(2)}) collective-permute-start(f32[2,128,256]{2,1,0:T(8,128)S(1)} %get-tuple-element.29), channel_id=1, source_target_pairs={{0,14},{1,15},{2,0},{3,1},{4,2},{5,3},{6,4},{7,5},{8,6},{9,7},{10,... | collective-permute-start | bytes 786440 | tf_op jit(solution)/shard_map/ppermute | solution.py:13
  132.1 10.7 %collective-permute-done.28 = f32[2,128,256]{2,1,0:T(8,128)S(1)} collective-permute-done((f32[2,128,256]{2,1,0:T(8,128)S(1)}, f32[2,128,256]{2,1,0:T(8,128)S(1)}, u32[]{:S(2)}, u32[]{:S(2)}) %collective-permute-start.28) | collective-permute-done | bytes 262176 | tf_op jit(solution)/shard_map/ppermute | solution.py:13
  142.8 3.4 collective-permute-start.33
  147.7 22.8 %collective-permute-start.35 = (f32[2,128,256]{2,1,0:T(8,128)S(1)}, f32[2,128,256]{2,1,0:T(8,128)S(1)}, u32[]{:S(2)}, u32[]{:S(2)}) collective-permute-start(f32[2,128,256]{2,1,0:T(8,128)S(1)} %get-tuple-element.25), channel_id=1, source_target_pairs={{0,10},{1,11},{2,12},{3,13},{4,14},{5,15},{6,0},{7,1},{8,2},{9,3},... | collective-permute-start | bytes 786440 | tf_op jit(solution)/shard_map/ppermute | solution.py:13
  170.6 3.3 collective-permute-done.34
  173.9 7.0 %collective-permute-done.35 = f32[2,128,256]{2,1,0:T(8,128)S(1)} collective-permute-done((f32[2,128,256]{2,1,0:T(8,128)S(1)}, f32[2,128,256]{2,1,0:T(8,128)S(1)}, u32[]{:S(2)}, u32[]{:S(2)}) %collective-permute-start.35) | collective-permute-done | bytes 262176 | tf_op jit(solution)/shard_map/ppermute | solution.py:13
  182.5 6.1 %scatter_fusion.1 = f32[8,128,256]{2,1,0:T(8,128)S(1)} fusion(f32[8,128,256]{2,1,0:T(8,128)S(1)} %convolution_add_fusion.2, s32[24]{0:T(128)S(1)} %select_n.145, f32[24,128,256]{2,1,0:T(8,128)} %bitcast.166), kind=kCustom, calls=%fused_computation.8 | custom fusion | flops 786432 | bytes 9437280 | tf_op jit(solution)/shard_map/scatter-add | solution.py:108
  190.1 2.9 gather_fusion.4
  195.6 4.1 %collective-permute-start.37 = (bf16[2,128,256]{2,1,0:T(8,128)(2,1)S(1)}, bf16[2,128,256]{2,1,0:T(8,128)(2,1)S(1)}, u32[]{:S(2)}, u32[]{:S(2)}) collective-permute-start(bf16[2,128,256]{2,1,0:T(8,128)(2,1)S(1)} %get-tuple-element.48), channel_id=1, source_target_pairs={{0,14},{1,15},{2,0},{3,1},{4,2},{5,3},{6,4},{7,5},{8,6},{9,7},{10,... | collective-permute-start | bytes 393224 | tf_op jit(solution)/shard_map/ppermute | solution.py:13
  199.7 3.8 %collective-permute-start.39 = (bf16[2,128,256]{2,1,0:T(8,128)(2,1)S(1)}, bf16[2,128,256]{2,1,0:T(8,128)(2,1)S(1)}, u32[]{:S(2)}, u32[]{:S(2)}) collective-permute-start(bf16[2,128,256]{2,1,0:T(8,128)(2,1)S(1)} %get-tuple-element.46), channel_id=1, source_target_pairs={{0,12},{1,13},{2,14},{3,15},{4,0},{5,1},{6,2},{7,3},{8,4},{9,5},{1... | collective-permute-start | bytes 393224 | tf_op jit(solution)/shard_map/ppermute | solution.py:13
  209.1 7.0 %collective-permute-start.44 = (bf16[2,128,256]{2,1,0:T(8,128)(2,1)S(1)}, bf16[2,128,256]{2,1,0:T(8,128)(2,1)S(1)}, u32[]{:S(2)}, u32[]{:S(2)}) collective-permute-start(bf16[2,128,256]{2,1,0:T(8,128)(2,1)S(1)} %get-tuple-element.41), channel_id=1, source_target_pairs={{0,3},{1,4},{2,5},{3,6},{4,7},{5,8},{6,9},{7,10},{8,11},{9,12},{10... | collective-permute-start | bytes 393224 | tf_op jit(solution)/shard_map/ppermute | solution.py:13
  219.4 8.8 %collective-permute-start.47 = (bf16[2,128,256]{2,1,0:T(8,128)(2,1)S(1)}, bf16[2,128,256]{2,1,0:T(8,128)(2,1)S(1)}, u32[]{:S(2)}, u32[]{:S(2)}) collective-permute-start(bf16[2,128,256]{2,1,0:T(8,128)(2,1)S(1)} %get-tuple-element.38), channel_id=1, source_target_pairs={{0,6},{1,7},{2,8},{3,9},{4,10},{5,11},{6,12},{7,13},{8,14},{9,15},... | collective-permute-start | bytes 393224 | tf_op jit(solution)/shard_map/ppermute | solution.py:13
  232.8 4.2 %gather_fusion.5 = bf16[64,128,256]{2,1,0:T(8,128)(2,1)} fusion(bf16[24,128,256]{2,1,0:T(8,128)(2,1)} %bitcast.51, s32[1024]{0:T(1024)S(1)} %pad_clamp_fusion), kind=kCustom, calls=%fused_computation.3.clone | custom fusion | bytes 8388864 | tf_op jit(solution)/shard_map/jit(_take)/gather | solution.py:85
  237.0 2.8 broadcast_select_fusion
  239.8 6.3 %convolution_bitcast_fusion = f32[8,128,256]{2,1,0:T(8,128)S(1)} fusion(bf16[8,8,128,256]{3,2,1,0:T(8,128)(2,1)S(1)} %bitcast.163, bf16[8,8,256,256]{3,2,1,0:T(8,128)(2,1)} %param.18), kind=kOutput, calls=%fused_computation.15 | convolution fusion | flops 1073741824 | bytes 13631488 | tf_op jit(solution)/shard_map/bkij,bkpj->bpi/dot_general | solution.py:92
  246.7 4.6 %fusion.4 = f32[8,128,8,256]{3,1,2,0:T(8,128)} fusion(bf16[8,8,256,256]{3,2,1,0:T(8,128)(2,1)S(1)} %bitcast.160, bf16[8,128,256]{2,1,0:T(8,128)(2,1)S(1)} %fusion.3), kind=kOutput, calls=%fused_computation.30 | convolution fusion | flops 1073741824 | bytes 17301504 | tf_op jit(solution)/shard_map/bkij,bpi->bkpj/dot_general | solution.py:99
  253.3 19.8 %scatter_fusion.2 = f32[24,128,256]{2,1,0:T(8,128)} fusion(f32[24,128,256]{2,1,0:T(8,128)} %broadcast.302, s32[64]{0:T(128)S(1)} %copy-done.15, f32[64,128,256]{2,1,0:T(8,128)} %bitcast.161), kind=kCustom, calls=%fused_computation.9 | custom fusion | flops 2097152 | bytes 25166080 | tf_op jit(solution)/shard_map/scatter-add | solution.py:102
  273.1 2.3 fusion.23
  277.2 2.3 collective-permute-start.49
  280.9 3.5 collective-permute-start.51
  287.3 3.6 %collective-permute-start.54 = (f32[2,128,256]{2,1,0:T(8,128)S(1)}, f32[2,128,256]{2,1,0:T(8,128)S(1)}, u32[]{:S(2)}, u32[]{:S(2)}) collective-permute-start(f32[2,128,256]{2,1,0:T(8,128)S(1)} %get-tuple-element.18), channel_id=1, source_target_pairs={{0,15},{1,0},{2,1},{3,2},{4,3},{5,4},{6,5},{7,6},{8,7},{9,8},{10,9... | collective-permute-start | bytes 786440 | tf_op jit(solution)/shard_map/ppermute | solution.py:13
  290.9 7.7 %collective-permute-start.55 = (f32[2,128,256]{2,1,0:T(8,128)S(1)}, f32[2,128,256]{2,1,0:T(8,128)S(1)}, u32[]{:S(2)}, u32[]{:S(2)}) collective-permute-start(f32[2,128,256]{2,1,0:T(8,128)S(1)} %get-tuple-element.17), channel_id=1, source_target_pairs={{0,14},{1,15},{2,0},{3,1},{4,2},{5,3},{6,4},{7,5},{8,6},{9,7},{10,... | collective-permute-start | bytes 786440 | tf_op jit(solution)/shard_map/ppermute | solution.py:13
  298.7 10.7 %collective-permute-done.52 = f32[2,128,256]{2,1,0:T(8,128)S(1)} collective-permute-done((f32[2,128,256]{2,1,0:T(8,128)S(1)}, f32[2,128,256]{2,1,0:T(8,128)S(1)}, u32[]{:S(2)}, u32[]{:S(2)}) %collective-permute-start.52) | collective-permute-done | bytes 262176 | tf_op jit(solution)/shard_map/ppermute | solution.py:13
  309.5 4.1 %collective-permute-start.57 = (f32[2,128,256]{2,1,0:T(8,128)S(1)}, f32[2,128,256]{2,1,0:T(8,128)S(1)}, u32[]{:S(2)}, u32[]{:S(2)}) collective-permute-start(f32[2,128,256]{2,1,0:T(8,128)S(1)} %get-tuple-element.15), channel_id=1, source_target_pairs={{0,12},{1,13},{2,14},{3,15},{4,0},{5,1},{6,2},{7,3},{8,4},{9,5},{1... | collective-permute-start | bytes 786440 | tf_op jit(solution)/shard_map/ppermute | solution.py:13
  313.7 20.4 %collective-permute-start.59 = (f32[2,128,256]{2,1,0:T(8,128)S(1)}, f32[2,128,256]{2,1,0:T(8,128)S(1)}, u32[]{:S(2)}, u32[]{:S(2)}) collective-permute-start(f32[2,128,256]{2,1,0:T(8,128)S(1)} %get-tuple-element.13), channel_id=1, source_target_pairs={{0,10},{1,11},{2,12},{3,13},{4,14},{5,15},{6,0},{7,1},{8,2},{9,3},... | collective-permute-start | bytes 786440 | tf_op jit(solution)/shard_map/ppermute | solution.py:13
  334.2 3.0 collective-permute-done.58
  337.3 7.2 %collective-permute-done.59 = f32[2,128,256]{2,1,0:T(8,128)S(1)} collective-permute-done((f32[2,128,256]{2,1,0:T(8,128)S(1)}, f32[2,128,256]{2,1,0:T(8,128)S(1)}, u32[]{:S(2)}, u32[]{:S(2)}) %collective-permute-start.59) | collective-permute-done | bytes 262176 | tf_op jit(solution)/shard_map/ppermute | solution.py:13
  346.1 6.1 %scatter_fusion.3 = f32[8,128,256]{2,1,0:T(8,128)S(1)} fusion(f32[8,128,256]{2,1,0:T(8,128)S(1)} %convolution_add_fusion, s32[24]{0:T(128)S(1)} %select_n.145, f32[24,128,256]{2,1,0:T(8,128)} %bitcast.167), kind=kCustom, calls=%fused_computation.10 | custom fusion | flops 786432 | bytes 9437280 | tf_op jit(solution)/shard_map/scatter-add | solution.py:108
  352.2 3.7 %multiply_add_fusion = (f32[8,128,256]{2,1,0:T(8,128)}, f32[8,128,256]{2,1,0:T(8,128)}, f32[8,128,256]{2,1,0:T(8,128)}) fusion(f32[8,128,256]{2,1,0:T(8,128)} %get-tuple-element.8, f32[128]{0:T(128)S(1)} %copy-done.17, f32[8,128,256]{2,1,0:T(8,128)S(1)} %scatter_fusion.3, f32[128]{0:T(128)S(1)} %copy-done.18, f32[8,128,256]{2,1,0:T(8,128)} %param.14, ...), kind=kLoop, calls=%fused_computation.25 | loop fusion | flops 2359296 | bytes 7341568 | tf_op jit(solution)/shard_map/add | solution.py:117
  (269 shorter events, 65.8 us)
Async XLA Ops:
  0.6 12.4 %collective-permute-start = (s32[8,8]{1,0:T(8,128)}, s32[8,8]{1,0:T(8,128)S(1)}, u32[]{:S(2)}, u32[]{:S(2)}) collective-permute-start(s32[8,8]{1,0:T(8,128)} %param.19), channel_id=1, source_target_pairs={{0,15},{1,0},{2,1},{3,2},{4,3},{5,4},{6,5},{7,6},{8,7},{9,8},{10,9... | collective-permute-start | bytes 776 | tf_op jit(solution)/shard_map/ppermute | solution.py:13
  1.5 12.8 %collective-permute-start.1 = (s32[8,8]{1,0:T(8,128)}, s32[8,8]{1,0:T(8,128)S(1)}, u32[]{:S(2)}, u32[]{:S(2)}) collective-permute-start(s32[8,8]{1,0:T(8,128)} %param.19), channel_id=1, source_target_pairs={{0,14},{1,15},{2,0},{3,1},{4,2},{5,3},{6,4},{7,5},{8,6},{9,7},{10,... | collective-permute-start | bytes 776 | tf_op jit(solution)/shard_map/ppermute | solution.py:13
  2.2 12.4 %collective-permute-start.2 = (s32[8,8]{1,0:T(8,128)}, s32[8,8]{1,0:T(8,128)S(1)}, u32[]{:S(2)}, u32[]{:S(2)}) collective-permute-start(s32[8,8]{1,0:T(8,128)} %param.19), channel_id=1, source_target_pairs={{0,13},{1,14},{2,15},{3,0},{4,1},{5,2},{6,3},{7,4},{8,5},{9,6},{10... | collective-permute-start | bytes 776 | tf_op jit(solution)/shard_map/ppermute | solution.py:13
  2.4 12.7 %collective-permute-start.3 = (s32[8,8]{1,0:T(8,128)}, s32[8,8]{1,0:T(8,128)S(1)}, u32[]{:S(2)}, u32[]{:S(2)}) collective-permute-start(s32[8,8]{1,0:T(8,128)} %param.19), channel_id=1, source_target_pairs={{0,12},{1,13},{2,14},{3,15},{4,0},{5,1},{6,2},{7,3},{8,4},{9,5},{1... | collective-permute-start | bytes 776 | tf_op jit(solution)/shard_map/ppermute | solution.py:13
  6.0 12.1 %collective-permute-start.4 = (s32[8,8]{1,0:T(8,128)}, s32[8,8]{1,0:T(8,128)S(1)}, u32[]{:S(2)}, u32[]{:S(2)}) collective-permute-start(s32[8,8]{1,0:T(8,128)} %param.19), channel_id=1, source_target_pairs={{0,11},{1,12},{2,13},{3,14},{4,15},{5,0},{6,1},{7,2},{8,3},{9,4},{... | collective-permute-start | bytes 776 | tf_op jit(solution)/shard_map/ppermute | solution.py:13
  33.3 11.4 %collective-permute-start.13 = (bf16[2,128,256]{2,1,0:T(8,128)(2,1)}, bf16[2,128,256]{2,1,0:T(8,128)(2,1)S(1)}, u32[]{:S(2)}, u32[]{:S(2)}) collective-permute-start(bf16[2,128,256]{2,1,0:T(8,128)(2,1)} %get-tuple-element.60), channel_id=1, source_target_pairs={{0,14},{1,15},{2,0},{3,1},{4,2},{5,3},{6,4},{7,5},{8,6},{9,7},{10,... | collective-permute-start | bytes 393224 | tf_op jit(solution)/shard_map/ppermute | solution.py:13
  36.6 9.2 %collective-permute-start.15 = (bf16[2,128,256]{2,1,0:T(8,128)(2,1)}, bf16[2,128,256]{2,1,0:T(8,128)(2,1)S(1)}, u32[]{:S(2)}, u32[]{:S(2)}) collective-permute-start(bf16[2,128,256]{2,1,0:T(8,128)(2,1)} %get-tuple-element.58), channel_id=1, source_target_pairs={{0,12},{1,13},{2,14},{3,15},{4,0},{5,1},{6,2},{7,3},{8,4},{9,5},{1... | collective-permute-start | bytes 393224 | tf_op jit(solution)/shard_map/ppermute | solution.py:13
  36.9 14.0 %collective-permute-start.16 = (bf16[2,128,256]{2,1,0:T(8,128)(2,1)}, bf16[2,128,256]{2,1,0:T(8,128)(2,1)S(1)}, u32[]{:S(2)}, u32[]{:S(2)}) collective-permute-start(bf16[2,128,256]{2,1,0:T(8,128)(2,1)} %get-tuple-element.57), channel_id=1, source_target_pairs={{0,11},{1,12},{2,13},{3,14},{4,15},{5,0},{6,1},{7,2},{8,3},{9,4},{... | collective-permute-start | bytes 393224 | tf_op jit(solution)/shard_map/ppermute | solution.py:13
  40.2 19.1 %collective-permute-start.17 = (bf16[2,128,256]{2,1,0:T(8,128)(2,1)}, bf16[2,128,256]{2,1,0:T(8,128)(2,1)S(1)}, u32[]{:S(2)}, u32[]{:S(2)}) collective-permute-start(bf16[2,128,256]{2,1,0:T(8,128)(2,1)} %get-tuple-element.56), channel_id=1, source_target_pairs={{0,10},{1,11},{2,12},{3,13},{4,14},{5,15},{6,0},{7,1},{8,2},{9,3},... | collective-permute-start | bytes 393224 | tf_op jit(solution)/shard_map/ppermute | solution.py:13
  44.7 14.6 %collective-permute-start.18 = (bf16[2,128,256]{2,1,0:T(8,128)(2,1)}, bf16[2,128,256]{2,1,0:T(8,128)(2,1)S(1)}, u32[]{:S(2)}, u32[]{:S(2)}) collective-permute-start(bf16[2,128,256]{2,1,0:T(8,128)(2,1)} %get-tuple-element.55), channel_id=1, source_target_pairs={{0,1},{1,2},{2,3},{3,4},{4,5},{5,6},{6,7},{7,8},{8,9},{9,10},{10,1... | collective-permute-start | bytes 393224 | tf_op jit(solution)/shard_map/ppermute | solution.py:13
  44.8 20.2 %collective-permute-start.19 = (bf16[2,128,256]{2,1,0:T(8,128)(2,1)}, bf16[2,128,256]{2,1,0:T(8,128)(2,1)S(1)}, u32[]{:S(2)}, u32[]{:S(2)}) collective-permute-start(bf16[2,128,256]{2,1,0:T(8,128)(2,1)} %get-tuple-element.54), channel_id=1, source_target_pairs={{0,2},{1,3},{2,4},{3,5},{4,6},{5,7},{6,8},{7,9},{8,10},{9,11},{10,... | collective-permute-start | bytes 393224 | tf_op jit(solution)/shard_map/ppermute | solution.py:13
  45.8 19.2 %collective-permute-start.20 = (bf16[2,128,256]{2,1,0:T(8,128)(2,1)}, bf16[2,128,256]{2,1,0:T(8,128)(2,1)S(1)}, u32[]{:S(2)}, u32[]{:S(2)}) collective-permute-start(bf16[2,128,256]{2,1,0:T(8,128)(2,1)} %get-tuple-element.53), channel_id=1, source_target_pairs={{0,3},{1,4},{2,5},{3,6},{4,7},{5,8},{6,9},{7,10},{8,11},{9,12},{10... | collective-permute-start | bytes 393224 | tf_op jit(solution)/shard_map/ppermute | solution.py:13
  50.8 14.2 %collective-permute-start.21 = (bf16[2,128,256]{2,1,0:T(8,128)(2,1)S(1)}, bf16[2,128,256]{2,1,0:T(8,128)(2,1)S(1)}, u32[]{:S(2)}, u32[]{:S(2)}) collective-permute-start(bf16[2,128,256]{2,1,0:T(8,128)(2,1)S(1)} %get-tuple-element.52), channel_id=1, source_target_pairs={{0,4},{1,5},{2,6},{3,7},{4,8},{5,9},{6,10},{7,11},{8,12},{9,13},{1... | collective-permute-start | bytes 393224 | tf_op jit(solution)/shard_map/ppermute | solution.py:13
  59.3 11.1 %collective-permute-start.23 = (bf16[2,128,256]{2,1,0:T(8,128)(2,1)S(1)}, bf16[2,128,256]{2,1,0:T(8,128)(2,1)S(1)}, u32[]{:S(2)}, u32[]{:S(2)}) collective-permute-start(bf16[2,128,256]{2,1,0:T(8,128)(2,1)S(1)} %get-tuple-element.50), channel_id=1, source_target_pairs={{0,6},{1,7},{2,8},{3,9},{4,10},{5,11},{6,12},{7,13},{8,14},{9,15},... | collective-permute-start | bytes 393224 | tf_op jit(solution)/shard_map/ppermute | solution.py:13
  111.6 10.1 %collective-permute-start.25 = (f32[2,128,256]{2,1,0:T(8,128)S(1)}, f32[2,128,256]{2,1,0:T(8,128)S(1)}, u32[]{:S(2)}, u32[]{:S(2)}) collective-permute-start(f32[2,128,256]{2,1,0:T(8,128)S(1)} %get-tuple-element.35), channel_id=1, source_target_pairs={{0,2},{1,3},{2,4},{3,5},{4,6},{5,7},{6,8},{7,9},{8,10},{9,11},{10,... | collective-permute-start | bytes 786440 | tf_op jit(solution)/shard_map/ppermute | solution.py:13
  113.9 11.5 %collective-permute-start.26 = (f32[2,128,256]{2,1,0:T(8,128)S(1)}, f32[2,128,256]{2,1,0:T(8,128)S(1)}, u32[]{:S(2)}, u32[]{:S(2)}) collective-permute-start(f32[2,128,256]{2,1,0:T(8,128)S(1)} %get-tuple-element.34), channel_id=1, source_target_pairs={{0,3},{1,4},{2,5},{3,6},{4,7},{5,8},{6,9},{7,10},{8,11},{9,12},{10... | collective-permute-start | bytes 786440 | tf_op jit(solution)/shard_map/ppermute | solution.py:13
  115.0 17.0 %collective-permute-start.27 = (f32[2,128,256]{2,1,0:T(8,128)S(1)}, f32[2,128,256]{2,1,0:T(8,128)S(1)}, u32[]{:S(2)}, u32[]{:S(2)}) collective-permute-start(f32[2,128,256]{2,1,0:T(8,128)S(1)} %get-tuple-element.33), channel_id=1, source_target_pairs={{0,4},{1,5},{2,6},{3,7},{4,8},{5,9},{6,10},{7,11},{8,12},{9,13},{1... | collective-permute-start | bytes 786440 | tf_op jit(solution)/shard_map/ppermute | solution.py:13
  118.8 24.0 %collective-permute-start.28 = (f32[2,128,256]{2,1,0:T(8,128)S(1)}, f32[2,128,256]{2,1,0:T(8,128)S(1)}, u32[]{:S(2)}, u32[]{:S(2)}) collective-permute-start(f32[2,128,256]{2,1,0:T(8,128)S(1)} %get-tuple-element.32), channel_id=1, source_target_pairs={{0,5},{1,6},{2,7},{3,8},{4,9},{5,10},{6,11},{7,12},{8,13},{9,14},{... | collective-permute-start | bytes 786440 | tf_op jit(solution)/shard_map/ppermute | solution.py:13
  120.5 25.8 %collective-permute-start.29 = (f32[2,128,256]{2,1,0:T(8,128)S(1)}, f32[2,128,256]{2,1,0:T(8,128)S(1)}, u32[]{:S(2)}, u32[]{:S(2)}) collective-permute-start(f32[2,128,256]{2,1,0:T(8,128)S(1)} %get-tuple-element.31), channel_id=1, source_target_pairs={{0,6},{1,7},{2,8},{3,9},{4,10},{5,11},{6,12},{7,13},{8,14},{9,15},... | collective-permute-start | bytes 786440 | tf_op jit(solution)/shard_map/ppermute | solution.py:13
  121.7 26.0 %collective-permute-start.30 = (f32[2,128,256]{2,1,0:T(8,128)S(1)}, f32[2,128,256]{2,1,0:T(8,128)S(1)}, u32[]{:S(2)}, u32[]{:S(2)}) collective-permute-start(f32[2,128,256]{2,1,0:T(8,128)S(1)} %get-tuple-element.30), channel_id=1, source_target_pairs={{0,15},{1,0},{2,1},{3,2},{4,3},{5,4},{6,5},{7,6},{8,7},{9,8},{10,9... | collective-permute-start | bytes 786440 | tf_op jit(solution)/shard_map/ppermute | solution.py:13
  125.4 45.1 %collective-permute-start.31 = (f32[2,128,256]{2,1,0:T(8,128)S(1)}, f32[2,128,256]{2,1,0:T(8,128)S(1)}, u32[]{:S(2)}, u32[]{:S(2)}) collective-permute-start(f32[2,128,256]{2,1,0:T(8,128)S(1)} %get-tuple-element.29), channel_id=1, source_target_pairs={{0,14},{1,15},{2,0},{3,1},{4,2},{5,3},{6,4},{7,5},{8,6},{9,7},{10,... | collective-permute-start | bytes 786440 | tf_op jit(solution)/shard_map/ppermute | solution.py:13
  132.0 38.5 %collective-permute-start.32 = (f32[2,128,256]{2,1,0:T(8,128)S(1)}, f32[2,128,256]{2,1,0:T(8,128)S(1)}, u32[]{:S(2)}, u32[]{:S(2)}) collective-permute-start(f32[2,128,256]{2,1,0:T(8,128)S(1)} %get-tuple-element.28), channel_id=1, source_target_pairs={{0,13},{1,14},{2,15},{3,0},{4,1},{5,2},{6,3},{7,4},{8,5},{9,6},{10... | collective-permute-start | bytes 786440 | tf_op jit(solution)/shard_map/ppermute | solution.py:13
  142.8 27.7 %collective-permute-start.33 = (f32[2,128,256]{2,1,0:T(8,128)S(1)}, f32[2,128,256]{2,1,0:T(8,128)S(1)}, u32[]{:S(2)}, u32[]{:S(2)}) collective-permute-start(f32[2,128,256]{2,1,0:T(8,128)S(1)} %get-tuple-element.27), channel_id=1, source_target_pairs={{0,12},{1,13},{2,14},{3,15},{4,0},{5,1},{6,2},{7,3},{8,4},{9,5},{1... | collective-permute-start | bytes 786440 | tf_op jit(solution)/shard_map/ppermute | solution.py:13
  146.3 27.6 %collective-permute-start.34 = (f32[2,128,256]{2,1,0:T(8,128)S(1)}, f32[2,128,256]{2,1,0:T(8,128)S(1)}, u32[]{:S(2)}, u32[]{:S(2)}) collective-permute-start(f32[2,128,256]{2,1,0:T(8,128)S(1)} %get-tuple-element.26), channel_id=1, source_target_pairs={{0,11},{1,12},{2,13},{3,14},{4,15},{5,0},{6,1},{7,2},{8,3},{9,4},{... | collective-permute-start | bytes 786440 | tf_op jit(solution)/shard_map/ppermute | solution.py:13
  147.7 33.2 %collective-permute-start.35 = (f32[2,128,256]{2,1,0:T(8,128)S(1)}, f32[2,128,256]{2,1,0:T(8,128)S(1)}, u32[]{:S(2)}, u32[]{:S(2)}) collective-permute-start(f32[2,128,256]{2,1,0:T(8,128)S(1)} %get-tuple-element.25), channel_id=1, source_target_pairs={{0,10},{1,11},{2,12},{3,13},{4,14},{5,15},{6,0},{7,1},{8,2},{9,3},... | collective-permute-start | bytes 786440 | tf_op jit(solution)/shard_map/ppermute | solution.py:13
  194.8 9.5 %collective-permute-start.36 = (bf16[2,128,256]{2,1,0:T(8,128)(2,1)S(1)}, bf16[2,128,256]{2,1,0:T(8,128)(2,1)S(1)}, u32[]{:S(2)}, u32[]{:S(2)}) collective-permute-start(bf16[2,128,256]{2,1,0:T(8,128)(2,1)S(1)} %get-tuple-element.49), channel_id=1, source_target_pairs={{0,15},{1,0},{2,1},{3,2},{4,3},{5,4},{6,5},{7,6},{8,7},{9,8},{10,9... | collective-permute-start | bytes 393224 | tf_op jit(solution)/shard_map/ppermute | solution.py:13
  195.6 9.7 %collective-permute-start.37 = (bf16[2,128,256]{2,1,0:T(8,128)(2,1)S(1)}, bf16[2,128,256]{2,1,0:T(8,128)(2,1)S(1)}, u32[]{:S(2)}, u32[]{:S(2)}) collective-permute-start(bf16[2,128,256]{2,1,0:T(8,128)(2,1)S(1)} %get-tuple-element.48), channel_id=1, source_target_pairs={{0,14},{1,15},{2,0},{3,1},{4,2},{5,3},{6,4},{7,5},{8,6},{9,7},{10,... | collective-permute-start | bytes 393224 | tf_op jit(solution)/shard_map/ppermute | solution.py:13
  199.7 9.4 %collective-permute-start.39 = (bf16[2,128,256]{2,1,0:T(8,128)(2,1)S(1)}, bf16[2,128,256]{2,1,0:T(8,128)(2,1)S(1)}, u32[]{:S(2)}, u32[]{:S(2)}) collective-permute-start(bf16[2,128,256]{2,1,0:T(8,128)(2,1)S(1)} %get-tuple-element.46), channel_id=1, source_target_pairs={{0,12},{1,13},{2,14},{3,15},{4,0},{5,1},{6,2},{7,3},{8,4},{9,5},{1... | collective-permute-start | bytes 393224 | tf_op jit(solution)/shard_map/ppermute | solution.py:13
  203.5 13.3 %collective-permute-start.40 = (bf16[2,128,256]{2,1,0:T(8,128)(2,1)S(1)}, bf16[2,128,256]{2,1,0:T(8,128)(2,1)S(1)}, u32[]{:S(2)}, u32[]{:S(2)}) collective-permute-start(bf16[2,128,256]{2,1,0:T(8,128)(2,1)S(1)} %get-tuple-element.45), channel_id=1, source_target_pairs={{0,11},{1,12},{2,13},{3,14},{4,15},{5,0},{6,1},{7,2},{8,3},{9,4},{... | collective-permute-start | bytes 393224 | tf_op jit(solution)/shard_map/ppermute | solution.py:13
  204.3 14.4 %collective-permute-start.41 = (bf16[2,128,256]{2,1,0:T(8,128)(2,1)S(1)}, bf16[2,128,256]{2,1,0:T(8,128)(2,1)S(1)}, u32[]{:S(2)}, u32[]{:S(2)}) collective-permute-start(bf16[2,128,256]{2,1,0:T(8,128)(2,1)S(1)} %get-tuple-element.44), channel_id=1, source_target_pairs={{0,10},{1,11},{2,12},{3,13},{4,14},{5,15},{6,0},{7,1},{8,2},{9,3},... | collective-permute-start | bytes 393224 | tf_op jit(solution)/shard_map/ppermute | solution.py:13
  205.3 14.1 %collective-permute-start.42 = (bf16[2,128,256]{2,1,0:T(8,128)(2,1)S(1)}, bf16[2,128,256]{2,1,0:T(8,128)(2,1)S(1)}, u32[]{:S(2)}, u32[]{:S(2)}) collective-permute-start(bf16[2,128,256]{2,1,0:T(8,128)(2,1)S(1)} %get-tuple-element.43), channel_id=1, source_target_pairs={{0,1},{1,2},{2,3},{3,4},{4,5},{5,6},{6,7},{7,8},{8,9},{9,10},{10,1... | collective-permute-start | bytes 393224 | tf_op jit(solution)/shard_map/ppermute | solution.py:13
  206.3 22.5 %collective-permute-start.43 = (bf16[2,128,256]{2,1,0:T(8,128)(2,1)S(1)}, bf16[2,128,256]{2,1,0:T(8,128)(2,1)S(1)}, u32[]{:S(2)}, u32[]{:S(2)}) collective-permute-start(bf16[2,128,256]{2,1,0:T(8,128)(2,1)S(1)} %get-tuple-element.42), channel_id=1, source_target_pairs={{0,2},{1,3},{2,4},{3,5},{4,6},{5,7},{6,8},{7,9},{8,10},{9,11},{10,... | collective-permute-start | bytes 393224 | tf_op jit(solution)/shard_map/ppermute | solution.py:13
  209.1 20.4 %collective-permute-start.44 = (bf16[2,128,256]{2,1,0:T(8,128)(2,1)S(1)}, bf16[2,128,256]{2,1,0:T(8,128)(2,1)S(1)}, u32[]{:S(2)}, u32[]{:S(2)}) collective-permute-start(bf16[2,128,256]{2,1,0:T(8,128)(2,1)S(1)} %get-tuple-element.41), channel_id=1, source_target_pairs={{0,3},{1,4},{2,5},{3,6},{4,7},{5,8},{6,9},{7,10},{8,11},{9,12},{10... | collective-permute-start | bytes 393224 | tf_op jit(solution)/shard_map/ppermute | solution.py:13
  216.7 13.4 %collective-permute-start.45 = (bf16[2,128,256]{2,1,0:T(8,128)(2,1)S(1)}, bf16[2,128,256]{2,1,0:T(8,128)(2,1)S(1)}, u32[]{:S(2)}, u32[]{:S(2)}) collective-permute-start(bf16[2,128,256]{2,1,0:T(8,128)(2,1)S(1)} %get-tuple-element.40), channel_id=1, source_target_pairs={{0,4},{1,5},{2,6},{3,7},{4,8},{5,9},{6,10},{7,11},{8,12},{9,13},{1... | collective-permute-start | bytes 393224 | tf_op jit(solution)/shard_map/ppermute | solution.py:13
  218.7 12.1 %collective-permute-start.46 = (bf16[2,128,256]{2,1,0:T(8,128)(2,1)S(1)}, bf16[2,128,256]{2,1,0:T(8,128)(2,1)S(1)}, u32[]{:S(2)}, u32[]{:S(2)}) collective-permute-start(bf16[2,128,256]{2,1,0:T(8,128)(2,1)S(1)} %get-tuple-element.39), channel_id=1, source_target_pairs={{0,5},{1,6},{2,7},{3,8},{4,9},{5,10},{6,11},{7,12},{8,13},{9,14},{... | collective-permute-start | bytes 393224 | tf_op jit(solution)/shard_map/ppermute | solution.py:13
  219.4 12.7 %collective-permute-start.47 = (bf16[2,128,256]{2,1,0:T(8,128)(2,1)S(1)}, bf16[2,128,256]{2,1,0:T(8,128)(2,1)S(1)}, u32[]{:S(2)}, u32[]{:S(2)}) collective-permute-start(bf16[2,128,256]{2,1,0:T(8,128)(2,1)S(1)} %get-tuple-element.38), channel_id=1, source_target_pairs={{0,6},{1,7},{2,8},{3,9},{4,10},{5,11},{6,12},{7,13},{8,14},{9,15},... | collective-permute-start | bytes 393224 | tf_op jit(solution)/shard_map/ppermute | solution.py:13
  275.4 9.4 %collective-permute-start.48 = (f32[2,128,256]{2,1,0:T(8,128)S(1)}, f32[2,128,256]{2,1,0:T(8,128)S(1)}, u32[]{:S(2)}, u32[]{:S(2)}) collective-permute-start(f32[2,128,256]{2,1,0:T(8,128)S(1)} %get-tuple-element.24), channel_id=1, source_target_pairs={{0,1},{1,2},{2,3},{3,4},{4,5},{5,6},{6,7},{7,8},{8,9},{9,10},{10,1... | collective-permute-start | bytes 786440 | tf_op jit(solution)/shard_map/ppermute | solution.py:13
  277.2 10.1 %collective-permute-start.49 = (f32[2,128,256]{2,1,0:T(8,128)S(1)}, f32[2,128,256]{2,1,0:T(8,128)S(1)}, u32[]{:S(2)}, u32[]{:S(2)}) collective-permute-start(f32[2,128,256]{2,1,0:T(8,128)S(1)} %get-tuple-element.23), channel_id=1, source_target_pairs={{0,2},{1,3},{2,4},{3,5},{4,6},{5,7},{6,8},{7,9},{8,10},{9,11},{10,... | collective-permute-start | bytes 786440 | tf_op jit(solution)/shard_map/ppermute | solution.py:13
  279.5 11.3 %collective-permute-start.50 = (f32[2,128,256]{2,1,0:T(8,128)S(1)}, f32[2,128,256]{2,1,0:T(8,128)S(1)}, u32[]{:S(2)}, u32[]{:S(2)}) collective-permute-start(f32[2,128,256]{2,1,0:T(8,128)S(1)} %get-tuple-element.22), channel_id=1, source_target_pairs={{0,3},{1,4},{2,5},{3,6},{4,7},{5,8},{6,9},{7,10},{8,11},{9,12},{10... | collective-permute-start | bytes 786440 | tf_op jit(solution)/shard_map/ppermute | solution.py:13
  280.9 17.7 %collective-permute-start.51 = (f32[2,128,256]{2,1,0:T(8,128)S(1)}, f32[2,128,256]{2,1,0:T(8,128)S(1)}, u32[]{:S(2)}, u32[]{:S(2)}) collective-permute-start(f32[2,128,256]{2,1,0:T(8,128)S(1)} %get-tuple-element.21), channel_id=1, source_target_pairs={{0,4},{1,5},{2,6},{3,7},{4,8},{5,9},{6,10},{7,11},{8,12},{9,13},{1... | collective-permute-start | bytes 786440 | tf_op jit(solution)/shard_map/ppermute | solution.py:13
  284.5 25.0 %collective-permute-start.52 = (f32[2,128,256]{2,1,0:T(8,128)S(1)}, f32[2,128,256]{2,1,0:T(8,128)S(1)}, u32[]{:S(2)}, u32[]{:S(2)}) collective-permute-start(f32[2,128,256]{2,1,0:T(8,128)S(1)} %get-tuple-element.20), channel_id=1, source_target_pairs={{0,5},{1,6},{2,7},{3,8},{4,9},{5,10},{6,11},{7,12},{8,13},{9,14},{... | collective-permute-start | bytes 786440 | tf_op jit(solution)/shard_map/ppermute | solution.py:13
  284.8 28.8 %collective-permute-start.53 = (f32[2,128,256]{2,1,0:T(8,128)S(1)}, f32[2,128,256]{2,1,0:T(8,128)S(1)}, u32[]{:S(2)}, u32[]{:S(2)}) collective-permute-start(f32[2,128,256]{2,1,0:T(8,128)S(1)} %get-tuple-element.19), channel_id=1, source_target_pairs={{0,6},{1,7},{2,8},{3,9},{4,10},{5,11},{6,12},{7,13},{8,14},{9,15},... | collective-permute-start | bytes 786440 | tf_op jit(solution)/shard_map/ppermute | solution.py:13
  287.3 26.4 %collective-permute-start.54 = (f32[2,128,256]{2,1,0:T(8,128)S(1)}, f32[2,128,256]{2,1,0:T(8,128)S(1)}, u32[]{:S(2)}, u32[]{:S(2)}) collective-permute-start(f32[2,128,256]{2,1,0:T(8,128)S(1)} %get-tuple-element.18), channel_id=1, source_target_pairs={{0,15},{1,0},{2,1},{3,2},{4,3},{5,4},{6,5},{7,6},{8,7},{9,8},{10,9... | collective-permute-start | bytes 786440 | tf_op jit(solution)/shard_map/ppermute | solution.py:13
  290.9 43.2 %collective-permute-start.55 = (f32[2,128,256]{2,1,0:T(8,128)S(1)}, f32[2,128,256]{2,1,0:T(8,128)S(1)}, u32[]{:S(2)}, u32[]{:S(2)}) collective-permute-start(f32[2,128,256]{2,1,0:T(8,128)S(1)} %get-tuple-element.17), channel_id=1, source_target_pairs={{0,14},{1,15},{2,0},{3,1},{4,2},{5,3},{6,4},{7,5},{8,6},{9,7},{10,... | collective-permute-start | bytes 786440 | tf_op jit(solution)/shard_map/ppermute | solution.py:13
  298.6 35.5 %collective-permute-start.56 = (f32[2,128,256]{2,1,0:T(8,128)S(1)}, f32[2,128,256]{2,1,0:T(8,128)S(1)}, u32[]{:S(2)}, u32[]{:S(2)}) collective-permute-start(f32[2,128,256]{2,1,0:T(8,128)S(1)} %get-tuple-element.16), channel_id=1, source_target_pairs={{0,13},{1,14},{2,15},{3,0},{4,1},{5,2},{6,3},{7,4},{8,5},{9,6},{10... | collective-permute-start | bytes 786440 | tf_op jit(solution)/shard_map/ppermute | solution.py:13
  309.5 24.7 %collective-permute-start.57 = (f32[2,128,256]{2,1,0:T(8,128)S(1)}, f32[2,128,256]{2,1,0:T(8,128)S(1)}, u32[]{:S(2)}, u32[]{:S(2)}) collective-permute-start(f32[2,128,256]{2,1,0:T(8,128)S(1)} %get-tuple-element.15), channel_id=1, source_target_pairs={{0,12},{1,13},{2,14},{3,15},{4,0},{5,1},{6,2},{7,3},{8,4},{9,5},{1... | collective-permute-start | bytes 786440 | tf_op jit(solution)/shard_map/ppermute | solution.py:13
  313.6 23.7 %collective-permute-start.58 = (f32[2,128,256]{2,1,0:T(8,128)S(1)}, f32[2,128,256]{2,1,0:T(8,128)S(1)}, u32[]{:S(2)}, u32[]{:S(2)}) collective-permute-start(f32[2,128,256]{2,1,0:T(8,128)S(1)} %get-tuple-element.14), channel_id=1, source_target_pairs={{0,11},{1,12},{2,13},{3,14},{4,15},{5,0},{6,1},{7,2},{8,3},{9,4},{... | collective-permute-start | bytes 786440 | tf_op jit(solution)/shard_map/ppermute | solution.py:13
  313.7 30.8 %collective-permute-start.59 = (f32[2,128,256]{2,1,0:T(8,128)S(1)}, f32[2,128,256]{2,1,0:T(8,128)S(1)}, u32[]{:S(2)}, u32[]{:S(2)}) collective-permute-start(f32[2,128,256]{2,1,0:T(8,128)S(1)} %get-tuple-element.13), channel_id=1, source_target_pairs={{0,10},{1,11},{2,12},{3,13},{4,14},{5,15},{6,0},{7,1},{8,2},{9,3},... | collective-permute-start | bytes 786440 | tf_op jit(solution)/shard_map/ppermute | solution.py:13
  (42 other events, 363.8 us)
where the time goes:
time: 360 us; the launch traced here: 356 us
  starting transfers between devices  153 us (42%)
  waiting for transfers between devices  69.1 us (19%)
  other arithmetic  68.5 us (19%)
  local copies, waits for them, and re-layouts  40.1 us (11%)
  matrix products  23.5 us (7%)
    ppermute x60, starting transfers between devices, shifted(): lax.ppermute(value, axis, [(i, (i + by) % length) for i in range(length)])  153 us
    ppermute x60, waiting for transfers between devices, shifted(): lax.ppermute(value, axis, [(i, (i + by) % length) for i in range(length)])  69.1 us
    scatter-add x2, other arithmetic, on_device(): jax.ops.segment_sum(partials.reshape(own_blocks * cond_count, probe_width...  39.6 us
    unnamed x116, local copies, waits for them, and re-layouts  12.9 us
    dot_general x2, matrix products, on_device(): jnp.einsum('bkij,bkpj->bpi', cond_blocks, remote, preferred_element_type=...  12.6 us
    scatter-add x2, other arithmetic, on_device(): jax.ops.segment_sum(returned.reshape(slot_groups * CAP, probe_width, poin...  12.1 us
    dot_general x2, matrix products, on_device(): jnp.einsum('bkij,bpi->bkpj', cond_blocks, scaled, preferred_element_type=...  9.25 us
  transfers between devices with their start and end apart: 60, of which 19 were waited for; matrix products, arithmetic and copies ran while one was open for 5% of the time, Pallas kernels for 0%

commit v1 on v0

v1 whole, which is shorter than its diff:
```python
import functools

import jax
import jax.numpy as jnp
from jax import lax
from jax.experimental import pallas as pl
from jax.experimental.pallas import tpu as pltpu
from jax.sharding import PartitionSpec as P

CAP = 2
RADIUS = 6
ITERS = 2
PEERS = 2 * RADIUS
MESH = pl.DeviceIdType.MESH

NT = (((1,), (1,)), ((), ()))
NN = (((1,), (0,)), ((), ()))


def offset_of(n):
    return (1 - 2 * (n % 2)) * (RADIUS - n // 2)


def kernel(
    dev_count, asked, entry, rhs, precision, hessian, alpha, beta, diag_hbm, cond_hbm,
    res_out, image_out,
    diag, cond, low, total, scaled, direc,
    pay, arr, ret, back,
    diag_sem, cond_sem, fsend, frecv, bsend, brecv,
):
    me = lax.axis_index("rows")
    own = rhs.shape[0]
    entries = cond_hbm.shape[0]

    def peer(n, sign):
        return lax.rem(me + sign * offset_of(n) + dev_count, dev_count)

    barrier = pltpu.get_barrier_semaphore()

    def greet(n, carry):
        pl.semaphore_signal(
            barrier, inc=1, device_id={"rows": peer(n, 1)}, device_id_type=MESH
        )
        return carry

    lax.fori_loop(0, PEERS, greet, 0)
    diag_copy = pltpu.make_async_copy(diag_hbm, diag, diag_sem)
    diag_copy.start()
    cond_copy = pltpu.make_async_copy(cond_hbm, cond.at[pl.ds(0, entries)], cond_sem)
    cond_copy.start()
    for b in range(own):
        low[b] = rhs[b].astype(jnp.bfloat16)
    cond[entries] = jnp.zeros(cond.shape[1:], cond.dtype)
    pl.semaphore_wait(barrier, PEERS)

    def fetch(t, n):
        return pltpu.make_async_remote_copy(
            src_ref=pay.at[t, n], dst_ref=arr.at[t, n],
            send_sem=fsend.at[t, n], recv_sem=frecv.at[t, n],
            device_id={"rows": peer(n, -1)}, device_id_type=MESH,
        )

    def give(t, n):
        return pltpu.make_async_remote_copy(
            src_ref=ret.at[t, n], dst_ref=back.at[t, n],
            send_sem=bsend.at[t, n], recv_sem=brecv.at[t, n],
            device_id={"rows": peer(n, 1)}, device_id_type=MESH,
        )

    for t in range(ITERS):
        def send_low(n, carry):
            for k in range(CAP):
                pay[t, n, k] = low[asked[n * CAP + k]]
            fetch(t, n).start()
            return carry

        lax.fori_loop(0, PEERS, send_low, 0)
        if t == 0:
            diag_copy.wait()

        def own_forward(b, carry):
            total[b] = lax.dot_general(low[b], diag[b], NT, preferred_element_type=jnp.float32)
            return carry

        lax.fori_loop(0, own, own_forward, 0)
        if t == 0:
            cond_copy.wait()

        def far_forward(n, carry):
            fetch(t, n).wait_recv()
            for b in range(own):
                acc = total[b]
                for k in range(CAP):
                    factor = cond[entry[(n * CAP + k) * own + b]]
                    acc = acc + lax.dot_general(
                        arr[t, n, k], factor, NT, preferred_element_type=jnp.float32
                    )
                total[b] = acc
            return carry

        lax.fori_loop(0, PEERS, far_forward, 0)
        for b in range(own):
            scaled[b] = (precision[b : b + 1, :] * total[b]).astype(jnp.bfloat16)

        def far_back(n, carry):
            for k in range(CAP):
                acc = jnp.zeros(total.shape[1:], jnp.float32)
                for b in range(own):
                    factor = cond[entry[(n * CAP + k) * own + b]]
                    acc = acc + lax.dot_general(
                        scaled[b], factor, NN, preferred_element_type=jnp.float32
                    )
                ret[t, n, k] = acc.astype(jnp.bfloat16)
            give(t, n).start()
            return carry

        lax.fori_loop(0, PEERS, far_back, 0)
        now = rhs if t == 0 else direc
        for b in range(own):
            image_out[b] = lax.dot_general(
                scaled[b], diag[b], NN, preferred_element_type=jnp.float32
            ) + hessian[b : b + 1, :] * now[b]

        def gather_back(n, carry):
            give(t, n).wait_recv()
            terms = [back[t, n, k].astype(jnp.float32) for k in range(CAP)]
            for b in range(own):
                acc = image_out[b]
                for k in range(CAP):
                    acc = acc + jnp.where(asked[n * CAP + k] == b, 1.0, 0.0) * terms[k]
                image_out[b] = acc
            return carry

        lax.fori_loop(0, PEERS, gather_back, 0)
        if t == 0:
            for b in range(own):
                left = rhs[b] - alpha[...] * image_out[b]
                res_out[b] = left
                new = left + beta[...] * rhs[b]
                direc[b] = new
                low[b] = new.astype(jnp.bfloat16)

    def drain(n, carry):
        for t in range(ITERS):
            fetch(t, n).wait_send()
            give(t, n).wait_send()
        return carry

    lax.fori_loop(0, PEERS, drain, 0)


def two_blocks(lists, owner, own):
    hit = lists // own == owner
    local = lists % own
    return (
        jnp.min(jnp.where(hit, local, own), axis=1),
        jnp.max(jnp.where(hit, local, -1), axis=1),
    )


def on_device(rhs, precision, hessian, diag_blocks, cond_blocks, cond_ids, step_alpha, step_beta):
    dev_count = lax.axis_size("rows")
    me = lax.axis_index("rows")
    own, probes, points = rhs.shape
    conds = cond_ids.shape[1]
    entries = own * conds
    flat = cond_ids.reshape(1, entries)
    everyone = lax.all_gather(flat[0], "rows")
    offsets = jnp.array([offset_of(n) for n in range(PEERS)], jnp.int32)
    owners = (me + offsets + dev_count) % dev_count
    listers = (me - offsets + dev_count) % dev_count

    lo, hi = two_blocks(flat, owners[:, None], own)
    second = jnp.where(hi > lo, hi, -1)
    local = jnp.stack([jnp.where(lo < own, lo, -1), second], axis=1)
    wanted = jnp.where(local >= 0, owners[:, None] * own + local, -1)
    same = wanted[:, :, None, None] == cond_ids[None, None, :, :]
    number = jnp.arange(entries, dtype=jnp.int32).reshape(own, conds)
    entry = jnp.min(jnp.where(same, number, entries), axis=3).reshape(-1)

    their_lo, their_hi = two_blocks(jnp.take(everyone, listers, axis=0), me, own)
    asked = jnp.stack([their_lo % own, jnp.maximum(their_hi, 0)], axis=1).reshape(-1)

    alpha0 = step_alpha[0][:, None]
    beta0 = step_beta[0][:, None]
    vmem = pl.BlockSpec(memory_space=pltpu.VMEM)
    smem = pl.BlockSpec(memory_space=pltpu.SMEM)
    hbm = pl.BlockSpec(memory_space=pl.ANY)
    low_type = jnp.bfloat16
    slots = (ITERS, PEERS, CAP, probes, points)
    res1, image1 = pl.pallas_call(
        functools.partial(kernel, dev_count),
        out_shape=[jax.ShapeDtypeStruct(rhs.shape, jnp.float32)] * 2,
        in_specs=[smem, smem, vmem, vmem, vmem, vmem, vmem, hbm, hbm],
        out_specs=[vmem, vmem],
        scratch_shapes=[
            pltpu.VMEM(diag_blocks.shape, low_type),
            pltpu.VMEM((entries + 1, points, points), low_type),
            pltpu.VMEM(rhs.shape, low_type),
            pltpu.VMEM(rhs.shape, jnp.float32),
            pltpu.VMEM(rhs.shape, low_type),
            pltpu.VMEM(rhs.shape, jnp.float32),
            pltpu.VMEM(slots, low_type),
            pltpu.VMEM(slots, low_type),
            pltpu.VMEM(slots, low_type),
            pltpu.VMEM(slots, low_type),
            pltpu.SemaphoreType.DMA,
            pltpu.SemaphoreType.DMA,
            pltpu.SemaphoreType.DMA((ITERS, PEERS)),
            pltpu.SemaphoreType.DMA((ITERS, PEERS)),
            pltpu.SemaphoreType.DMA((ITERS, PEERS)),
            pltpu.SemaphoreType.DMA((ITERS, PEERS)),
        ],
        compiler_params=pltpu.CompilerParams(
            collective_id=0, has_side_effects=True, vmem_limit_bytes=48 * 1024 * 1024
        ),
    )(
        asked, entry, rhs, precision, hessian, alpha0, beta0,
        diag_blocks, cond_blocks.reshape(entries, points, points),
    )
    alpha1 = step_alpha[1][None, :, None]
    beta1 = step_beta[1][None, :, None]
    dir1 = res1 + beta0[None] * rhs
    sol = alpha0[None] * rhs + alpha1 * dir1
    res = res1 - alpha1 * image1
    return (sol, res, res + beta1 * dir1)


def solution(mesh):
    in_specs = (
        P(("groups", "rows"), None, None),
        P(("groups", "rows"), None),
        P(("groups", "rows"), None),
        P(("groups", "rows"), None, None),
        P(("groups", "rows"), None, None, None),
        P(("groups", "rows"), None),
        P(),
        P(),
    )
    out_specs = (
        P(("groups", "rows"), None, None),
        P(("groups", "rows"), None, None),
        P(("groups", "rows"), None, None),
    )
    return jax.shard_map(
        on_device, mesh=mesh, in_specs=in_specs, out_specs=out_specs, check_vma=False
    )
```

time: 360 us -> 167 us (0.46)
  starting transfers between devices: 153 us -> 0 us
  Pallas kernels: 0 us -> 138 us
  waiting for transfers between devices: 69.1 us -> 0 us
  other arithmetic: 68.5 us -> 4.8 us
  local copies, waits for them, and re-layouts: 40.1 us -> 7.28 us
  matrix products: 23.5 us -> 0 us
  blocking collectives: 0 us -> 15.9 us
    ppermute x60 -> x0, starting transfers between devices: 153 us -> none  [shifted(): lax.ppermute(value, axis, [(i, (i + by) % length) for i in range(length)])]
    pallas_call x0 -> x1, Pallas kernels: none -> 138 us  [on_device(): pl.pallas_call(functools.partial(kernel, dev_count), out_shape=[jax.Shape...]
    ppermute x60 -> x0, waiting for transfers between devices: 69.1 us -> none  [shifted(): lax.ppermute(value, axis, [(i, (i + by) % length) for i in range(length)])]
    scatter-add x4 -> x0, other arithmetic: 51.7 us -> none  [the longest x2 39.6 us: on_device(): jax.ops.segment_sum(partials.reshape(own_blocks * cond_count, probe_width...]
    dot_general x8 -> x0, matrix products: 23.5 us -> none  [the longest x2 12.6 us: on_device(): jnp.einsum('bkij,bkpj->bpi', cond_blocks, remote, preferred_element_type=...]
    all_gather x0 -> x1, blocking collectives: none -> 15.9 us  [on_device(): everyone = lax.all_gather(flat[0], 'rows')]
    gather x6 -> x1, local copies, waits for them, and re-layouts: 11.9 us -> 0.56 us  [on_device(): jnp.take(everyone, listers, axis=0)]
    unnamed x116 -> x9, local copies, waits for them, and re-layouts: 12.9 us -> 4.61 us
  transfers between devices with their start and end apart: 60 -> 0, of which waited for: 19 -> 0; matrix products, arithmetic and copies ran while one was open for 5% -> 0% of each run, Pallas kernels for 0% -> 0%
where the time goes in v1:
time: 167 us; the launch traced here: 166 us
  Pallas kernels  138 us (83%)
  blocking collectives  15.9 us (10%)
  local copies, waits for them, and re-layouts  7.28 us (4%)
  other arithmetic  4.8 us (3%)
    pallas_call x1, Pallas kernels, on_device(): pl.pallas_call(functools.partial(kernel, dev_count), out_shape=[jax.Shape...  138 us
    all_gather x1, blocking collectives, on_device(): everyone = lax.all_gather(flat[0], 'rows')  15.9 us
    unnamed x9, local copies, waits for them, and re-layouts  4.61 us

profile of v1, /device:TPU:18, one launch (start us, length us, event | category | flops | bytes accessed | tf_op | source)
XLA Modules:
  0.0 166.2 jit_solution(18218754896847805384)
XLA Ops:
  0.6 0.8 reshape.252
  1.4 0.8 all_gather_squeeze_reshape.6
  2.2 0.7 broadcast_multiply_fusion
  2.9 0.2 fusion
  3.1 0.7 compare_and_fusion
  3.7 0.8 slice_bitcast_fusion
  4.5 0.8 select_reduce_fusion
  5.3 0.1 copy.27
  5.4 0.1 reshape.241.entry
  5.5 15.9 %all-gather = s32[16,1,64]{2,1,0:T(1,128)S(1)} all-gather(s32[1,1,64]{2,1,0:T(1,128)S(1)} %reshape.252), channel_id=1, replica_groups=mesh['groups'=2,'rows'=16] {'rows'}, dimensions={0}, use_global_device_ids=true | all-gather | bytes 4352 | tf_op jit(solution)/shard_map/all_gather | solution.py:168
  21.4 0.6 gather_fusion
  22.0 0.2 select_reduce_fusion.2
  22.2 0.1 copy.26
  22.3 0.1 reshape.237.asked
  22.4 0.1 copy.29.beta
  22.5 0.1 copy.28.alpha
  22.6 0.0 copy-start
  22.7 1.2 copy-done
  23.9 0.0 copy-start.1
  23.9 1.2 copy-done.1
  25.1 0.0 copy-start.2
  25.1 0.7 copy-done.2
  25.8 0.0 copy-start.3
  25.8 0.7 copy-done.3
  26.5 137.5 %shard_map.112 = (f32[8,128,256]{2,1,0:T(8,128)S(1)}, f32[8,128,256]{2,1,0:T(8,128)S(1)}) custom-call(s32[24]{0:T(128)S(1)} %reshape.237.asked, s32[192]{0:T(256)S(1)} %reshape.241.entry, f32[8,128,256]{2,1,0:T(8,128)S(1)} %copy-done, f32[8,256]{1,0:T(8,128)S(1)} %copy-done.2, f32[8,256]{1,0:T(8,128)S(1)} %copy-done.3, f32[128,1]{1,0:T(8,128)S(1)} %copy.28.alpha, ...), custom_call_target="tpu_custom_call" | custom-call | tf_op jit(solution)/shard_map/pallas_call | solution.py:191
  164.0 2.2 %multiply_add_fusion = (f32[8,128,256]{2,1,0:T(8,128)}, f32[8,128,256]{2,1,0:T(8,128)}, f32[8,128,256]{2,1,0:T(8,128)}) fusion(f32[128]{0:T(128)S(1)} %get-tuple-element.18, f32[8,128,256]{2,1,0:T(8,128)S(1)} %get-tuple-element.5, f32[8,128,256]{2,1,0:T(8,128)S(1)} %copy-done, f32[128]{0:T(128)S(1)} %get-tuple-element.19, ...), kind=kLoop, calls=%fused_computation.1 | loop fusion | flops 2359296 | bytes 6293504 | tf_op jit(solution)/shard_map/add | solution.py:226
  (8 shorter events, 0.1 us)
Async XLA Ops:
  22.6 1.2 copy-start
  23.9 1.2 copy-start.1
  25.1 0.7 copy-start.2
  25.8 0.7 copy-start.3

commit v2 on v1

v2 whole, which is shorter than its diff:
```python
import functools

import jax
import jax.numpy as jnp
from jax import lax
from jax.experimental import pallas as pl
from jax.experimental.pallas import tpu as pltpu
from jax.sharding import PartitionSpec as P

CAP = 2
RADIUS = 6
ITERS = 2
PEERS = 2 * RADIUS
MESH = pl.DeviceIdType.MESH

NT = (((1,), (1,)), ((), ()))
NN = (((1,), (0,)), ((), ()))


def offset_of(n):
    return (1 - 2 * (n % 2)) * (RADIUS - n // 2)


def kernel(
    dev_count, ids, alpha_rows, beta_rows,
    rhs_hbm, precision_hbm, hessian_hbm, diag_hbm, cond_hbm,
    res_out, image_out,
    rhs, precision, hessian, diag, cond, low, total, scaled, direc, alpha, beta,
    want, got, entry_rows, got_smem, entry_smem,
    pay, arr, ret, back,
    local_sem, smem_sem, wsend, wrecv, fsend, frecv, bsend, brecv,
):
    me = lax.axis_index("rows")
    own, probes, points = rhs.shape
    entries = cond_hbm.shape[0]
    conds = entries // own

    def peer(n, sign):
        return lax.rem(me + sign * offset_of(n) + dev_count, dev_count)

    barrier = pltpu.get_barrier_semaphore()

    def greet(n, carry):
        pl.semaphore_signal(
            barrier, inc=1, device_id={"rows": peer(n, 1)}, device_id_type=MESH
        )
        return carry

    lax.fori_loop(0, PEERS, greet, 0)
    pairs = [
        (rhs_hbm, rhs), (precision_hbm, precision), (hessian_hbm, hessian), (diag_hbm, diag),
        (cond_hbm, cond.at[pl.ds(0, entries)]),
    ]
    loads = [
        pltpu.make_async_copy(source, target, local_sem.at[number])
        for number, (source, target) in enumerate(pairs)
    ]
    for load in loads:
        load.start()

    lane = lax.broadcasted_iota(jnp.int32, (16, 128), 1)
    slot = lax.broadcasted_iota(jnp.int32, (16, 128), 0)
    distance = (1 - 2 * (slot & 1)) * (RADIUS - (slot >> 1))
    owner = me + distance
    owner = jnp.where(owner < 0, owner + dev_count, owner)
    owner = jnp.where(owner >= dev_count, owner - dev_count, owner)
    listed = ids[0:1, :] - owner * own
    hit = (listed >= 0) & (listed < own)
    lowest = jnp.min(jnp.where(hit, listed, own), axis=1, keepdims=True)
    highest = jnp.max(jnp.where(hit, listed, -1), axis=1, keepdims=True)
    first = jnp.where(lowest < own, lowest, -1)
    second = jnp.where(highest > lowest, highest, -1)
    rows = jnp.where(lane == 0, first, jnp.where(lane == 1, second, 0))
    for n in range(PEERS):
        want[n] = rows[n : n + 1, :]
    pl.semaphore_wait(barrier, PEERS)

    def tell(n):
        return pltpu.make_async_remote_copy(
            src_ref=want.at[n], dst_ref=got.at[n],
            send_sem=wsend.at[n], recv_sem=wrecv.at[n],
            device_id={"rows": peer(n, 1)}, device_id_type=MESH,
        )

    def start_tell(n, carry):
        tell(n).start()
        return carry

    def wait_tell(n, carry):
        tell(n).wait_recv()
        return carry

    lax.fori_loop(0, PEERS, start_tell, 0)
    loads[0].wait()
    for b in range(own):
        low[b] = rhs[b].astype(jnp.bfloat16)
    lax.fori_loop(0, PEERS, wait_tell, 0)
    asked_copy = pltpu.make_async_copy(got, got_smem, smem_sem.at[0])
    asked_copy.start()
    asked_copy.wait()

    def asked(n, k):
        return got_smem[n, 0, k]

    def entry(n, k, b):
        return entry_smem[n * CAP + k, 0, b]

    def prepare():
        column = lax.broadcasted_iota(jnp.int32, (conds, 128), 1)
        number = column * conds + lax.broadcasted_iota(jnp.int32, (conds, 128), 0)
        by_row = ids[8 : 8 + conds, :]
        for n in range(PEERS):
            base = owner[n : n + 1, :] * own
            for k, local in enumerate((first, second)):
                mine = local[n : n + 1, :]
                block = jnp.where(mine >= 0, base + mine, -2)
                found = jnp.where((by_row == block) & (column < own), number, entries)
                entry_rows[n * CAP + k] = jnp.min(found, axis=0, keepdims=True)
        entry_copy = pltpu.make_async_copy(entry_rows, entry_smem, smem_sem.at[1])
        entry_copy.start()
        for rows_ref, full in ((alpha_rows, alpha), (beta_rows, beta)):
            spread = jnp.transpose(jnp.broadcast_to(rows_ref[0:1, :], (128, probes)))
            for part in range(points // 128):
                full[:, part * 128 : (part + 1) * 128] = spread
        cond[entries] = jnp.zeros(cond.shape[1:], cond.dtype)
        for load in loads[1:4]:
            load.wait()
        entry_copy.wait()

    def fetch(t, n):
        return pltpu.make_async_remote_copy(
            src_ref=pay.at[t, n], dst_ref=arr.at[t, n],
            send_sem=fsend.at[t, n], recv_sem=frecv.at[t, n],
            device_id={"rows": peer(n, -1)}, device_id_type=MESH,
        )

    def give(t, n):
        return pltpu.make_async_remote_copy(
            src_ref=ret.at[t, n], dst_ref=back.at[t, n],
            send_sem=bsend.at[t, n], recv_sem=brecv.at[t, n],
            device_id={"rows": peer(n, 1)}, device_id_type=MESH,
        )

    for t in range(ITERS):
        def send_low(n, carry):
            for k in range(CAP):
                pay[t, n, k] = low[jnp.maximum(asked(n, k), 0)]
            fetch(t, n).start()
            return carry

        lax.fori_loop(0, PEERS, send_low, 0)
        if t == 0:
            prepare()

        def own_forward(b, carry):
            total[b] = lax.dot_general(low[b], diag[b], NT, preferred_element_type=jnp.float32)
            return carry

        lax.fori_loop(0, own, own_forward, 0)
        if t == 0:
            loads[4].wait()

        def far_forward(n, carry):
            fetch(t, n).wait_recv()
            for b in range(own):
                acc = total[b]
                for k in range(CAP):
                    factor = cond[entry(n, k, b)]
                    acc = acc + lax.dot_general(
                        arr[t, n, k], factor, NT, preferred_element_type=jnp.float32
                    )
                total[b] = acc
            return carry

        lax.fori_loop(0, PEERS, far_forward, 0)
        for b in range(own):
            scaled[b] = (precision[b : b + 1, :] * total[b]).astype(jnp.bfloat16)

        def far_back(n, carry):
            for k in range(CAP):
                acc = jnp.zeros(total.shape[1:], jnp.float32)
                for b in range(own):
                    factor = cond[entry(n, k, b)]
                    acc = acc + lax.dot_general(
                        scaled[b], factor, NN, preferred_element_type=jnp.float32
                    )
                ret[t, n, k] = acc.astype(jnp.bfloat16)
            give(t, n).start()
            return carry

        lax.fori_loop(0, PEERS, far_back, 0)
        now = rhs if t == 0 else direc
        for b in range(own):
            image_out[b] = lax.dot_general(
                scaled[b], diag[b], NN, preferred_element_type=jnp.float32
            ) + hessian[b : b + 1, :] * now[b]

        def gather_back(n, carry):
            give(t, n).wait_recv()
            terms = [back[t, n, k].astype(jnp.float32) for k in range(CAP)]
            for b in range(own):
                acc = image_out[b]
                for k in range(CAP):
                    acc = acc + jnp.where(asked(n, k) == b, 1.0, 0.0) * terms[k]
                image_out[b] = acc
            return carry

        lax.fori_loop(0, PEERS, gather_back, 0)
        if t == 0:
            for b in range(own):
                left = rhs[b] - alpha[...] * image_out[b]
                res_out[b] = left
                new = left + beta[...] * rhs[b]
                direc[b] = new
                low[b] = new.astype(jnp.bfloat16)

    def drain(n, carry):
        tell(n).wait_send()
        for t in range(ITERS):
            fetch(t, n).wait_send()
            give(t, n).wait_send()
        return carry

    lax.fori_loop(0, PEERS, drain, 0)


def on_device(rhs, precision, hessian, diag_blocks, cond_blocks, cond_ids, step_alpha, step_beta):
    dev_count = lax.axis_size("rows")
    own, probes, points = rhs.shape
    conds = cond_ids.shape[1]
    entries = own * conds
    flat = jnp.pad(cond_ids.reshape(1, entries), ((0, 7), (0, 128 - entries)), constant_values=-1)
    by_row = jnp.pad(cond_ids.T, ((0, 0), (0, 128 - own)), constant_values=-1)
    ids = jnp.concatenate([flat, by_row], axis=0)
    vmem = pl.BlockSpec(memory_space=pltpu.VMEM)
    hbm = pl.BlockSpec(memory_space=pl.ANY)
    low_type = jnp.bfloat16
    slots = (ITERS, PEERS, CAP, probes, points)
    res1, image1 = pl.pallas_call(
        functools.partial(kernel, dev_count),
        out_shape=[jax.ShapeDtypeStruct(rhs.shape, jnp.float32)] * 2,
        in_specs=[vmem] * 3 + [hbm] * 5,
        out_specs=[vmem, vmem],
        scratch_shapes=[
            pltpu.VMEM(rhs.shape, jnp.float32),
            pltpu.VMEM(precision.shape, jnp.float32),
            pltpu.VMEM(hessian.shape, jnp.float32),
            pltpu.VMEM(diag_blocks.shape, low_type),
            pltpu.VMEM((entries + 1, points, points), low_type),
            pltpu.VMEM(rhs.shape, low_type),
            pltpu.VMEM(rhs.shape, jnp.float32),
            pltpu.VMEM(rhs.shape, low_type),
            pltpu.VMEM(rhs.shape, jnp.float32),
            pltpu.VMEM((probes, points), jnp.float32),
            pltpu.VMEM((probes, points), jnp.float32),
            pltpu.VMEM((PEERS, 1, 128), jnp.int32),
            pltpu.VMEM((PEERS, 1, 128), jnp.int32),
            pltpu.VMEM((PEERS * CAP, 1, 128), jnp.int32),
            pltpu.SMEM((PEERS, 1, 128), jnp.int32),
            pltpu.SMEM((PEERS * CAP, 1, 128), jnp.int32),
            pltpu.VMEM(slots, low_type),
            pltpu.VMEM(slots, low_type),
            pltpu.VMEM(slots, low_type),
            pltpu.VMEM(slots, low_type),
            pltpu.SemaphoreType.DMA((5,)),
            pltpu.SemaphoreType.DMA((2,)),
            pltpu.SemaphoreType.DMA((PEERS,)),
            pltpu.SemaphoreType.DMA((PEERS,)),
            pltpu.SemaphoreType.DMA((ITERS, PEERS)),
            pltpu.SemaphoreType.DMA((ITERS, PEERS)),
            pltpu.SemaphoreType.DMA((ITERS, PEERS)),
            pltpu.SemaphoreType.DMA((ITERS, PEERS)),
        ],
        compiler_params=pltpu.CompilerParams(
            collective_id=0, has_side_effects=True, vmem_limit_bytes=56 * 1024 * 1024
        ),
    )(
        ids, step_alpha, step_beta, rhs, precision, hessian, diag_blocks,
        cond_blocks.reshape(entries, points, points),
    )
    alpha0 = step_alpha[0][None, :, None]
    beta0 = step_beta[0][None, :, None]
    alpha1 = step_alpha[1][None, :, None]
    beta1 = step_beta[1][None, :, None]
    dir1 = res1 + beta0 * rhs
    sol = alpha0 * rhs + alpha1 * dir1
    res = res1 - alpha1 * image1
    return (sol, res, res + beta1 * dir1)


def solution(mesh):
    in_specs = (
        P(("groups", "rows"), None, None),
        P(("groups", "rows"), None),
        P(("groups", "rows"), None),
        P(("groups", "rows"), None, None),
        P(("groups", "rows"), None, None, None),
        P(("groups", "rows"), None),
        P(),
        P(),
    )
    out_specs = (
        P(("groups", "rows"), None, None),
        P(("groups", "rows"), None, None),
        P(("groups", "rows"), None, None),
    )
    return jax.shard_map(
        on_device, mesh=mesh, in_specs=in_specs, out_specs=out_specs, check_vma=False
    )
```

time: 167 us -> 147 us (0.88)
  blocking collectives: 15.9 us -> 0 us
  local copies, waits for them, and re-layouts: 7.28 us -> 2.38 us
    all_gather x1 -> x0, blocking collectives: 15.9 us -> none  [on_device(): everyone = lax.all_gather(flat[0], 'rows')]
    unnamed x9 -> x3, local copies, waits for them, and re-layouts: 4.61 us -> 0.76 us
where the time goes in v2:
time: 147 us; the launch traced here: 145 us
  Pallas kernels  137 us (93%)
  other arithmetic  4.34 us (3%)
  local copies, waits for them, and re-layouts  2.38 us (2%)
    pallas_call x1, Pallas kernels, on_device(): pl.pallas_call(functools.partial(kernel, dev_count), out_shape=[jax.Shape...  137 us
    add x1, other arithmetic, on_device(): return (sol, res, res + beta1 * dir1)  3.74 us

profile of v2, /device:TPU:18, one launch (start us, length us, event | category | flops | bytes accessed | tf_op | source)
XLA Modules:
  0.0 144.9 jit_solution(7755853851352636861)
XLA Ops:
  0.6 0.0 copy-start
  0.6 0.9 reshape.16
  1.5 0.8 slice_bitcast_fusion
  2.3 0.8 copy.11
  3.0 0.6 select_add_fusion.ids
  3.6 137.5 %shard_map.103 = (f32[8,128,256]{2,1,0:T(8,128)}, f32[8,128,256]{2,1,0:T(8,128)}) custom-call(s32[16,128]{1,0:T(8,128)} %select_add_fusion.ids, f32[2,128]{1,0:T(2,128)} %alpha_rows.1, f32[2,128]{1,0:T(2,128)} %beta_rows.1, f32[8,128,256]{2,1,0:T(8,128)} %rhs_hbm.1, f32[8,256]{1,0:T(8,128)} %precision_hbm.1, f32[8,256]{1,0:T(8,128)} %hessian_hbm.1, ...), custom_call_target="tpu_custom_call" | custom-call | tf_op jit(solution)/shard_map/pallas_call | solution.py:239
  141.1 0.0 copy-done
  141.1 3.7 %multiply_add_fusion = (f32[8,128,256]{2,1,0:T(8,128)}, f32[8,128,256]{2,1,0:T(8,128)}, f32[8,128,256]{2,1,0:T(8,128)}) fusion(f32[128]{0:T(128)S(1)} %get-tuple-element.10, f32[8,128,256]{2,1,0:T(8,128)} %get-tuple-element.5, f32[8,128,256]{2,1,0:T(8,128)S(1)} %copy-done, f32[128]{0:T(128)S(1)} %get-tuple-element.11, f32[8,128,256]{2,1,0:T(8,128)} %get-tuple-element.6, ...), kind=kLoop, calls=%fused_computation | loop fusion | flops 2359296 | bytes 6293504 | tf_op jit(solution)/shard_map/add | solution.py:288
Async XLA Ops:
  0.6 140.5 %copy-start = (f32[8,128,256]{2,1,0:T(8,128)S(1)}, f32[8,128,256]{2,1,0:T(8,128)}, u32[]{:S(2)}) copy-start(f32[8,128,256]{2,1,0:T(8,128)} %rhs_hbm.1) | copy-start | bytes 3145732

commit v3 on v2

--- a/solution.py
+++ b/solution.py
@@ -18,7 +18,7 @@
 
 
 def offset_of(n):
-    return (1 - 2 * (n % 2)) * (RADIUS - n // 2)
+    return (1 - 2 * (n % 2)) * (RADIUS * (1 - n // 2 % 2) + n // 2 % 2 + (2 * (n // 2 % 2) - 1) * (n // 4))
 
 
 def kernel(
@@ -58,21 +58,18 @@
     for load in loads:
         load.start()
 
-    lane = lax.broadcasted_iota(jnp.int32, (16, 128), 1)
-    slot = lax.broadcasted_iota(jnp.int32, (16, 128), 0)
-    distance = (1 - 2 * (slot & 1)) * (RADIUS - (slot >> 1))
-    owner = me + distance
-    owner = jnp.where(owner < 0, owner + dev_count, owner)
-    owner = jnp.where(owner >= dev_count, owner - dev_count, owner)
-    listed = ids[0:1, :] - owner * own
-    hit = (listed >= 0) & (listed < own)
-    lowest = jnp.min(jnp.where(hit, listed, own), axis=1, keepdims=True)
-    highest = jnp.max(jnp.where(hit, listed, -1), axis=1, keepdims=True)
-    first = jnp.where(lowest < own, lowest, -1)
-    second = jnp.where(highest > lowest, highest, -1)
-    rows = jnp.where(lane == 0, first, jnp.where(lane == 1, second, 0))
+    lane = lax.broadcasted_iota(jnp.int32, (1, 128), 1)
+    chosen = []
     for n in range(PEERS):
-        want[n] = rows[n : n + 1, :]
+        base = peer(n, 1) * own
+        listed = ids[...] - base
+        hit = (listed >= 0) & (listed < own)
+        lowest = jnp.min(jnp.where(hit, listed, own), axis=(0, 1), keepdims=True)
+        highest = jnp.max(jnp.where(hit, listed, -1), axis=(0, 1), keepdims=True)
+        first = jnp.where(lowest < own, lowest, -1)
+        second = jnp.where(highest > lowest, highest, -1)
+        chosen.append((base, first, second))
+        want[n] = jnp.where(lane == 0, first, jnp.where(lane == 1, second, 0))
     pl.semaphore_wait(barrier, PEERS)
 
     def tell(n):
@@ -103,19 +100,20 @@
         return got_smem[n, 0, k]
 
     def entry(n, k, b):
-        return entry_smem[n * CAP + k, 0, b]
+        return entry_smem[b, n * CAP + k]
 
     def prepare():
-        column = lax.broadcasted_iota(jnp.int32, (conds, 128), 1)
-        number = column * conds + lax.broadcasted_iota(jnp.int32, (conds, 128), 0)
-        by_row = ids[8 : 8 + conds, :]
-        for n in range(PEERS):
-            base = owner[n : n + 1, :] * own
-            for k, local in enumerate((first, second)):
-                mine = local[n : n + 1, :]
+        number = lax.broadcasted_iota(jnp.int32, (own, conds), 0) * conds
+        number = number + lax.broadcasted_iota(jnp.int32, (own, conds), 1)
+        column = lax.broadcasted_iota(jnp.int32, (own, 128), 1)
+        table = jnp.full((own, 128), entries, jnp.int32)
+        for n, (base, *locals_) in enumerate(chosen):
+            for k, mine in enumerate(locals_):
                 block = jnp.where(mine >= 0, base + mine, -2)
-                found = jnp.where((by_row == block) & (column < own), number, entries)
-                entry_rows[n * CAP + k] = jnp.min(found, axis=0, keepdims=True)
+                found = jnp.where(ids[...] == block, number, entries)
+                least = jnp.min(found, axis=1, keepdims=True)
+                table = jnp.where(column == n * CAP + k, least, table)
+        entry_rows[...] = table
         entry_copy = pltpu.make_async_copy(entry_rows, entry_smem, smem_sem.at[1])
         entry_copy.start()
         for rows_ref, full in ((alpha_rows, alpha), (beta_rows, beta)):
@@ -229,9 +227,6 @@
     own, probes, points = rhs.shape
     conds = cond_ids.shape[1]
     entries = own * conds
-    flat = jnp.pad(cond_ids.reshape(1, entries), ((0, 7), (0, 128 - entries)), constant_values=-1)
-    by_row = jnp.pad(cond_ids.T, ((0, 0), (0, 128 - own)), constant_values=-1)
-    ids = jnp.concatenate([flat, by_row], axis=0)
     vmem = pl.BlockSpec(memory_space=pltpu.VMEM)
     hbm = pl.BlockSpec(memory_space=pl.ANY)
     low_type = jnp.bfloat16
@@ -255,9 +250,9 @@
             pltpu.VMEM((probes, points), jnp.float32),
             pltpu.VMEM((PEERS, 1, 128), jnp.int32),
             pltpu.VMEM((PEERS, 1, 128), jnp.int32),
-            pltpu.VMEM((PEERS * CAP, 1, 128), jnp.int32),
+            pltpu.VMEM((own, 128), jnp.int32),
             pltpu.SMEM((PEERS, 1, 128), jnp.int32),
-            pltpu.SMEM((PEERS * CAP, 1, 128), jnp.int32),
+            pltpu.SMEM((own, 128), jnp.int32),
             pltpu.VMEM(slots, low_type),
             pltpu.VMEM(slots, low_type),
             pltpu.VMEM(slots, low_type),
@@ -275,7 +270,7 @@
             collective_id=0, has_side_effects=True, vmem_limit_bytes=56 * 1024 * 1024
         ),
     )(
-        ids, step_alpha, step_beta, rhs, precision, hessian, diag_blocks,
+        cond_ids, step_alpha, step_beta, rhs, precision, hessian, diag_blocks,
         cond_blocks.reshape(entries, points, points),
     )
     alpha0 = step_alpha[0][None, :, None]

time: 147 us -> 143 us (0.973)
  Pallas kernels: 137 us -> 135 us
  local copies, waits for them, and re-layouts: 2.38 us -> 0.83 us
    pallas_call x1, Pallas kernels: 137 us -> 135 us  [on_device(): pl.pallas_call(functools.partial(kernel, dev_count), out_shape=[jax.Shape...]
where the time goes in v3:
time: 143 us; the launch traced here: 141 us
  Pallas kernels  135 us (94%)
  other arithmetic  3.73 us (3%)
    pallas_call x1, Pallas kernels, on_device(): pl.pallas_call(functools.partial(kernel, dev_count), out_shape=[jax.Shape...  135 us
    add x1, other arithmetic, on_device(): return (sol, res, res + beta1 * dir1)  3.73 us

profile of v3, /device:TPU:18, one launch (start us, length us, event | category | flops | bytes accessed | tf_op | source)
XLA Modules:
  0.0 140.6 jit_solution(12596790341694571040)
XLA Ops:
  0.6 0.0 copy-start
  0.6 0.8 slice_bitcast_fusion
  1.5 135.4 %shard_map.103 = (f32[8,128,256]{2,1,0:T(8,128)}, f32[8,128,256]{2,1,0:T(8,128)}) custom-call(s32[8,8]{1,0:T(8,128)} %ids.1, f32[2,128]{1,0:T(2,128)} %alpha_rows.1, f32[2,128]{1,0:T(2,128)} %beta_rows.1, f32[8,128,256]{2,1,0:T(8,128)} %rhs_hbm.1, f32[8,256]{1,0:T(8,128)} %precision_hbm.1, f32[8,256]{1,0:T(8,128)} %hessian_hbm.1, ...), custom_call_target="tpu_custom_call" | custom-call | tf_op jit(solution)/shard_map/pallas_call | solution.py:234
  136.8 0.0 copy-done
  136.8 3.7 %multiply_add_fusion = (f32[8,128,256]{2,1,0:T(8,128)}, f32[8,128,256]{2,1,0:T(8,128)}, f32[8,128,256]{2,1,0:T(8,128)}) fusion(f32[128]{0:T(128)S(1)} %get-tuple-element.10, f32[8,128,256]{2,1,0:T(8,128)} %get-tuple-element.5, f32[8,128,256]{2,1,0:T(8,128)S(1)} %copy-done, f32[128]{0:T(128)S(1)} %get-tuple-element.11, f32[8,128,256]{2,1,0:T(8,128)} %get-tuple-element.6, ...), kind=kLoop, calls=%fused_computation | loop fusion | flops 2359296 | bytes 6293504 | tf_op jit(solution)/shard_map/add | solution.py:283
Async XLA Ops:
  0.6 136.2 %copy-start = (f32[8,128,256]{2,1,0:T(8,128)S(1)}, f32[8,128,256]{2,1,0:T(8,128)}, u32[]{:S(2)}) copy-start(f32[8,128,256]{2,1,0:T(8,128)} %rhs_hbm.1) | copy-start | bytes 3145732

commit v4 on v3

--- a/solution.py
+++ b/solution.py
@@ -267,7 +267,7 @@
             pltpu.SemaphoreType.DMA((ITERS, PEERS)),
         ],
         compiler_params=pltpu.CompilerParams(
-            collective_id=0, has_side_effects=True, vmem_limit_bytes=56 * 1024 * 1024
+            collective_id=0, has_side_effects=True, vmem_limit_bytes=40 * 1024 * 1024
         ),
     )(
         cond_ids, step_alpha, step_beta, rhs, precision, hessian, diag_blocks,

time: 143 us -> 150 us (1.049)
  local copies, waits for them, and re-layouts: 0.83 us -> 10 us
  other arithmetic: 3.73 us -> 2.22 us
    unnamed x2 -> x16, local copies, waits for them, and re-layouts: 0.01 us -> 9.27 us
    add x1, other arithmetic: 3.73 us -> 2.22 us  [on_device(): return (sol, res, res + beta1 * dir1)]
where the time goes in v4:
time: 150 us; the launch traced here: 147 us
  Pallas kernels  134 us (89%)
  local copies, waits for them, and re-layouts  10 us (7%)
  other arithmetic  2.22 us (1%)
    pallas_call x1, Pallas kernels, on_device(): pl.pallas_call(functools.partial(kernel, dev_count), out_shape=[jax.Shape...  134 us
    unnamed x16, local copies, waits for them, and re-layouts  9.27 us

profile of v4, /device:TPU:18, one launch (start us, length us, event | category | flops | bytes accessed | tf_op | source)
XLA Modules:
  0.0 146.9 jit_solution(1501307174314448030)
XLA Ops:
  0.6 0.8 slice_bitcast_fusion
  1.4 0.0 copy-start
  1.4 3.4 %copy-done = bf16[8,8,256,256]{3,2,1,0:T(8,128)(2,1)S(1)} copy-done((bf16[8,8,256,256]{3,2,1,0:T(8,128)(2,1)S(1)}, bf16[8,8,256,256]{3,2,1,0:T(8,128)(2,1)}, u32[]{:S(2)}) %copy-start) | copy-done | bytes 8388632
  4.8 0.0 copy-start.1
  4.8 1.2 copy-done.1
  6.0 0.0 copy-start.2
  6.0 1.2 copy-done.2
  7.2 0.0 copy-start.3
  7.2 0.7 copy-done.3
  7.9 0.0 copy-start.4
  7.9 0.7 copy-done.4
  8.6 0.0 copy-start.5
  8.6 0.7 copy-done.5
  9.3 0.0 copy-start.6
  9.3 0.7 copy-done.6
  10.0 0.0 copy-start.7
  10.0 0.7 copy-done.7
  10.7 134.0 %shard_map.103 = (f32[8,128,256]{2,1,0:T(8,128)S(1)}, f32[8,128,256]{2,1,0:T(8,128)S(1)}) custom-call(s32[8,8]{1,0:T(8,128)S(1)} %copy-done.5, f32[2,128]{1,0:T(2,128)S(1)} %copy-done.7, f32[2,128]{1,0:T(2,128)S(1)} %copy-done.6, f32[8,128,256]{2,1,0:T(8,128)S(1)} %copy-done.1, f32[8,256]{1,0:T(8,128)S(1)} %copy-done.3, f32[8,256]{1,0:T(8,128)S(1)} %copy-done.4, ...), custom_call_target="tpu_custom_call" | custom-call | tf_op jit(solution)/shard_map/pallas_call | solution.py:234
  144.6 2.2 %multiply_add_fusion = (f32[8,128,256]{2,1,0:T(8,128)}, f32[8,128,256]{2,1,0:T(8,128)}, f32[8,128,256]{2,1,0:T(8,128)}) fusion(f32[128]{0:T(128)S(1)} %get-tuple-element.10, f32[8,128,256]{2,1,0:T(8,128)S(1)} %get-tuple-element.5, f32[8,128,256]{2,1,0:T(8,128)S(1)} %copy-done.1, f32[128]{0:T(128)S(1)} %get-tuple-element.11, ...), kind=kLoop, calls=%fused_computation | loop fusion | flops 2359296 | bytes 6293504 | tf_op jit(solution)/shard_map/add | solution.py:283
Async XLA Ops:
  1.4 3.4 %copy-start = (bf16[8,8,256,256]{3,2,1,0:T(8,128)(2,1)S(1)}, bf16[8,8,256,256]{3,2,1,0:T(8,128)(2,1)}, u32[]{:S(2)}) copy-start(bf16[8,8,256,256]{3,2,1,0:T(8,128)(2,1)} %param.12) | copy-start | bytes 25165828
  4.8 1.2 copy-start.1
  6.0 1.2 copy-start.2
  7.2 0.7 copy-start.3
  7.9 0.7 copy-start.4
  8.6 0.7 copy-start.5
  9.3 0.7 copy-start.6
  10.0 0.7 copy-start.7
